TPU v7x, 32 devices: a whole 2x2x4 slice. The times are simulated.
32 devices in a mesh: tile: 8 (over y, x, core), chan: 4 (over z).
Axes of the slice: x: 2, y: 2, z: 4, core: 2. Of those that a mesh axis runs over, the one named last changes fastest.
Arguments:
- latlon: bfloat16 [1, 2048, 8, 512], P(None, 'tile', None, 'chan'), may hold values from -6 to 6
- remap_weights: bfloat16 [8, 1156, 2048], P('tile'), may hold values from -0.1875 to 0.1875
- term_source: int32 [8, 256], replicated, may hold values from 0 to 7, as said below
- term_block: int32 [8, 256], replicated, may hold values from 0 to 255
- term_count: int32 [8], replicated, may hold values from 0 to 256, as said below
- rotation: int32 [8], P('tile'), may hold values from 0 to 3
- depthwise: bfloat16 [3, 3, 512], P(None, None, 'chan'), may hold values from -2 to 2
- pointwise: bfloat16 [512, 512], replicated, may hold values from -0.25 to 0.25
- cotangent: bfloat16 [1, 8192, 512], P(None, 'tile', 'chan'), may hold values from -6 to 6
Outputs:
- coupled: bfloat16 [1, 8192, 512], P(None, 'tile', 'chan')
- grad_latlon: bfloat16 [1, 2048, 8, 512], P(None, 'tile', None, 'chan')
- grad_depthwise: float32 [3, 3, 512], P(None, None, 'chan')
- grad_pointwise: float32 [512, 512], P('chan')
Inputs may be any that keep to these rules, and one draw needn't show every extreme that they name: `term_source`: the first term_count[d] entries of row d name the source tile of each term and the rest are 0. Among the used entries of a row no source tile appears more than 48 times, and some row names a tile exactly 48 times. `term_count`: some face tile uses all 256 terms.
All inputs are finite; a program needn't handle non-finite values.
Results may differ from a plain program's by a relative error of at most 0.0059.
Values may be sent and summed in bfloat16 or wider, within the bound.
A program may use at most 64 MiB of HBM per device.

v0:
```python
import math

import jax
import jax.numpy as jnp
from jax import lax
from jax.sharding import PartitionSpec as P

TILE_EDGE = 32


def turn_kernel(kernel, turn, direction):
    turned = jnp.zeros_like(kernel)
    for quarter in range(4):
        turned = turned + jnp.where(
            turn == quarter, jnp.rot90(kernel, direction * quarter, axes=(0, 1)), 0.0
        )
    return turned


def stencil_apply(field, kernel):
    shape_out = (field.shape[0], TILE_EDGE, TILE_EDGE, field.shape[3])
    hidden = jnp.zeros(shape_out, jnp.float32)
    for row_off in range(3):
        for col_off in range(3):
            window = field[
                :, row_off : row_off + TILE_EDGE, col_off : col_off + TILE_EDGE, :
            ].astype(jnp.float32)
            hidden = hidden + kernel[row_off, col_off] * window
    return hidden


def stencil_grads(field, kernel, grad_hidden):
    tap_rows = []
    grad_field = jnp.zeros(field.shape, jnp.float32)
    for row_off in range(3):
        tap_cols = []
        for col_off in range(3):
            window = field[
                :, row_off : row_off + TILE_EDGE, col_off : col_off + TILE_EDGE, :
            ].astype(jnp.float32)
            tap_cols.append(jnp.sum(window * grad_hidden, axis=(0, 1, 2)))
            spread = kernel[row_off, col_off] * grad_hidden
            grad_field = grad_field + jnp.pad(
                spread, ((0, 0), (row_off, 2 - row_off), (col_off, 2 - col_off), (0, 0))
            )
        tap_rows.append(jnp.stack(tap_cols))
    return (jnp.stack(tap_rows), grad_field)


def body(
    latlon,
    remap_weights,
    term_source,
    term_block,
    term_count,
    rotation,
    depthwise,
    pointwise,
    cotangent,
):
    tile_now = lax.axis_index("tile")
    tile_total = lax.axis_size("tile")
    chan_now = lax.axis_index("chan")
    batch_rows, block_total, seg_len, chan_local = latlon.shape
    terms_max = term_source.shape[1]
    capacity = 3 * terms_max // (2 * tile_total)
    ext_edge = TILE_EDGE + 2
    tile_cells = TILE_EDGE * TILE_EDGE
    flat_rows = batch_rows * tile_cells
    positions = jnp.arange(terms_max, dtype=jnp.int32)
    in_use = positions[None, :] < term_count[:, None]
    mine = in_use & (term_source == tile_now)
    send_rank = jnp.cumsum(mine.astype(jnp.int32), axis=1) - 1
    slot_ids = jnp.arange(capacity, dtype=jnp.int32)
    slot_hits = mine[:, :, None] & (send_rank[:, :, None] == slot_ids[None, None, :])
    slot_filled = jnp.any(slot_hits, axis=1).reshape(-1)
    slot_block = jnp.sum(jnp.where(slot_hits, term_block[:, :, None], 0), axis=1).reshape(-1)
    outgoing = jnp.take(latlon, slot_block, axis=1)
    outgoing = jnp.where(slot_filled[None, :, None, None], outgoing, jnp.zeros((), latlon.dtype))
    own_source = lax.dynamic_index_in_dim(term_source, tile_now, 0, keepdims=False)
    own_count = lax.dynamic_index_in_dim(term_count, tile_now, 0, keepdims=False)
    own_use = positions < own_count
    same_source = (
        (own_source[None, :] == own_source[:, None])
        & own_use[None, :]
        & (positions[None, :] <= positions[:, None])
    )
    own_rank = jnp.sum(same_source.astype(jnp.int32), axis=1) - 1
    recv_slot = jnp.where(own_use, own_source * capacity + own_rank, 0)
    return_slot = jnp.where(own_use, own_source * capacity + own_rank, tile_total * capacity)
    weights = remap_weights[0]
    ext_cells = weights.shape[0]
    term_pts = weights.shape[1]
    arrived = lax.all_to_all(outgoing, "tile", split_axis=1, concat_axis=1, tiled=True)
    picked = jnp.take(arrived, recv_slot, axis=1)
    picked = jnp.where(own_use[None, :, None, None], picked, jnp.zeros((), arrived.dtype))
    picked = picked.reshape(picked.shape[0], term_pts, chan_local)
    mapped = jnp.einsum("pk,bkc->bpc", weights, picked, preferred_element_type=jnp.float32)
    remapped = mapped.astype(jnp.bfloat16)
    field = remapped.reshape(batch_rows, ext_edge, ext_edge, chan_local)
    turn = rotation[0]
    kernel = turn_kernel(depthwise.astype(jnp.float32), turn, 1)
    hidden = stencil_apply(field, kernel)
    active = jax.nn.silu(hidden).astype(jnp.bfloat16).reshape(flat_rows, chan_local)
    own_rows = lax.dynamic_slice_in_dim(pointwise, chan_now * chan_local, chan_local, 0)
    partial_mix = jnp.dot(active, own_rows, preferred_element_type=jnp.float32)
    mixed = lax.psum_scatter(partial_mix, "chan", scatter_dimension=1, tiled=True)
    coupled = mixed.astype(jnp.bfloat16).reshape(batch_rows, tile_cells, chan_local)
    upstream = cotangent.reshape(flat_rows, chan_local)
    piece = lax.all_gather(upstream, "chan", axis=1, tiled=True)
    grad_active = lax.dot_general(
        piece, own_rows, (((1,), (1,)), ((), ())), preferred_element_type=jnp.float32
    )
    block_grad = lax.dot_general(
        active, piece, (((0,), (0,)), ((), ())), preferred_element_type=jnp.float32
    )
    grad_mix = block_grad
    grad_active, grad_mix = (grad_active, grad_mix)
    sigma = jax.nn.sigmoid(hidden)
    grad_hidden = grad_active.reshape(hidden.shape) * sigma * (1.0 + hidden * (1.0 - sigma))
    grad_turned, grad_field = stencil_grads(field, kernel, grad_hidden)
    grad_field = grad_field.astype(jnp.bfloat16).reshape(batch_rows, ext_cells, chan_local)
    grad_terms = jnp.einsum("pk,bpc->bkc", weights, grad_field, preferred_element_type=jnp.float32)
    grad_terms = grad_terms.reshape(batch_rows, terms_max, seg_len, chan_local)
    grad_terms = jnp.where(own_use[None, :, None, None], grad_terms, 0.0).astype(jnp.bfloat16)
    returning = jnp.zeros((batch_rows, tile_total * capacity, seg_len, chan_local), jnp.bfloat16)
    returning = returning.at[:, return_slot].set(grad_terms, mode="drop")
    landing = jnp.where(slot_filled, slot_block, block_total)
    arrived = lax.all_to_all(returning, "tile", split_axis=1, concat_axis=1, tiled=True)
    summed = jnp.zeros((arrived.shape[0], block_total, seg_len, chan_local), jnp.float32)
    summed = summed.at[:, landing].add(arrived.astype(jnp.float32), mode="drop")
    grad_latlon = summed.astype(jnp.bfloat16)
    grad_kernel = turn_kernel(grad_turned, turn, -1)
    kernel_sum, mix_sum = lax.psum((grad_kernel, grad_mix), "tile")
    factor = 1.0 / math.sqrt(batch_rows * tile_cells * tile_total)
    return (coupled, grad_latlon, kernel_sum * factor, mix_sum * factor)


def solution(mesh):
    return jax.shard_map(
        body,
        mesh=mesh,
        in_specs=(
            P(None, "tile", None, "chan"),
            P("tile", None, None),
            P(),
            P(),
            P(),
            P("tile"),
            P(None, None, "chan"),
            P(),
            P(None, "tile", "chan"),
        ),
        out_specs=(
            P(None, "tile", "chan"),
            P(None, "tile", None, "chan"),
            P(None, None, "chan"),
            P("chan", None),
        ),
        check_vma=False,
    )
```

profile of v0, /device:TPU:0, one launch (start us, length us, event | category | flops | bytes accessed | tf_op | source)
XLA Modules:
  0.0 168.0 jit_solution(11309757945237269254)
XLA Ops:
  9.2 0.9 select_reduce_fusion
  10.5 1.7 %gather_fusion = bf16[384,8,128]{2,1,0:T(8,128)(2,1)S(1)} fusion(bf16[256,8,128]{2,1,0:T(8,128)(2,1)S(1)} %bitcast.128, s32[1024]{0:T(1024)S(1)} %pad_clamp_fusion.1), kind=kCustom, calls=%fused_computation | custom fusion | bytes 1574400 | tf_op jit(solution)/shard_map/jit(_take)/gather | solution.py:78
  12.3 3.1 %fusion.17 = bf16[1,384,8,128]{3,2,0,1:T(8,128)(2,1)} fusion(bf16[384,8,128]{2,1,0:T(8,128)(2,1)S(1)} %gather_fusion, pred[384]{0:T(512)(128)(4,1)S(1)} %compare_and_fusion, pred[384]{0:T(512)(128)(4,1)S(1)} %broadcast_in_dim.109), kind=kLoop, calls=%fused_computation.19 | loop fusion | flops 786432 | bytes 1573632 | tf_op jit(solution)/shard_map/jit(_where)/select_n | solution.py:79
  15.4 5.2 %all-to-all-start = ((bf16[1,384,8,128]{3,2,0,1:T(8,128)(2,1)}), bf16[1,384,8,128]{3,2,0,1:T(8,128)(2,1)S(1)}, u32[]{:S(2)}, u32[]{:S(2)}) async-start(bf16[1,384,8,128]{3,2,0,1:T(8,128)(2,1)} %fusion.17), calls=%async_computation | async-start | bytes 1572864 | tf_op jit(solution)/shard_map/all_to_all | solution.py:94
  23.5 1.4 compare_select_fusion.2
  26.3 6.9 %all-to-all-done = bf16[1,384,8,128]{3,2,0,1:T(8,128)(2,1)S(1)} async-done(((bf16[1,384,8,128]{3,2,0,1:T(8,128)(2,1)}), bf16[1,384,8,128]{3,2,0,1:T(8,128)(2,1)S(1)}, u32[]{:S(2)}, u32[]{:S(2)}) %all-to-all-start) | async-done | bytes 786464 | tf_op jit(solution)/shard_map/all_to_all | solution.py:94
  34.0 3.9 %fusion.10 = bf16[1,1156,128]{2,1,0:T(8,128)(2,1)S(1)} fusion(bf16[1,1156,2048]{2,1,0:T(8,128)(2,1)} %param.10, bf16[256,8,128]{2,1,0:T(8,128)(2,1)S(1)} %gather_fusion.1, pred[256]{0:T(512)(128)(4,1)S(1)} %compare_and_fusion.1, pred[256]{0:T(512)(128)(4,1)S(1)} %iota_compare_fusion.3), kind=kOutput, calls=%fused_computation.10 | convolution fusion | flops 606749184 | bytes 5555712 | tf_op jit(solution)/shard_map/pk,bkc->bpc/dot_general | solution.py:98
  38.0 16.9 %all-gather.3.cloned.1.call-done = bf16[1,1024,512]{2,1,0:T(8,128)(2,1)} async-done(((bf16[1,1024,128]{2,1,0:T(8,128)(2,1)}), bf16[1,1024,512]{2,1,0:T(8,128)(2,1)}) %all-gather.3.cloned.1.call-update) | async-done | bytes 1048592 | tf_op jit(solution)/shard_map/all_gather | solution.py:110
  54.9 1.8 %convolution_bitcast_fusion = f32[1024,128]{0,1:T(8,128)S(1)} fusion(bf16[1,1024,512]{2,1,0:T(8,128)(2,1)} %all-gather.3.cloned.1.call-done, bf16[512,512]{1,0:T(8,128)(2,1)} %param.16, s32[]{:T(128)S(6)} %select_n.251), kind=kOutput, calls=%fused_computation.11 | convolution fusion | flops 134217728 | bytes 1703940 | tf_op jit(solution)/shard_map/dot_general | solution.py:111
  56.9 0.9 fusion.26
  57.8 1.8 %broadcast_multiply_fusion.8 = (f32[1,32,32,128]{3,2,1,0:T(8,128)S(1)}, f32[1,32,32,128]{3,2,1,0:T(8,128)S(1)}, f32[1,32,32,128]{3,2,1,0:T(8,128)S(1)}, f32[1,32...) fusion(f32[1,32,32,128]{3,2,1,0:T(8,128)S(1)} %get-tuple-elemen, ...), kind=kLoop, calls=%fused_computation.83 | loop fusion | flops 1835008 | bytes 6033920 | tf_op jit(solution)/shard_map/mul | solution.py:42
  59.6 1.0 fusion.14
  60.7 2.7 %fusion.47 = f32[1024,512]{1,0:T(8,128)} fusion(bf16[1024,128]{1,0:T(8,128)(2,1)S(1)} %bitcast.130, bf16[512,512]{1,0:T(8,128)(2,1)} %param.16, s32[]{:T(128)S(6)} %select_n.251), kind=kOutput, calls=%fused_computation.87 | convolution fusion | flops 134217728 | bytes 2490372 | tf_op jit(solution)/shard_map/dot_general | solution.py:106
  63.5 2.8 %add_convert_fusion = bf16[1,34,34,128]{3,2,1,0:T(8,128)(2,1)} fusion(f32[1,32,32,128]{3,2,1,0:T(8,128)S(1)} %get-tuple-element.36, f32[1,32,32,128]{3,2,1,0:T(8,128)S(1)} %get-tuple-element.37, f32[1,32,32,128]{3,2,1,0:T(8,128)S(1)} %get-tuple-element.38, f32[1,32,32,128]{3,2,1,0:T(8,128)S(1)} %get-tuple-element.39, ...), kind=kLoop, calls=%fused_computation.20 | loop fusion | flops 1331712 | bytes 5014528 | tf_op jit(solution)/shard_map/convert_element_type | solution.py:122
  66.3 1.1 reshape.359
  67.4 3.3 %fusion.4 = bf16[1,2048,128]{1,2,0:T(8,128)(2,1)S(1)} fusion(bf16[1156,128]{1,0:T(8,128)(2,1)S(1)} %reshape.359, bf16[1,1156,2048]{2,1,0:T(8,128)(2,1)} %param.10), kind=kOutput, calls=%fused_computation.8 | convolution fusion | flops 606076928 | bytes 5555200 | tf_op jit(solution)/shard_map/pk,bpc->bkc/dot_general | solution.py:123
  71.3 1.0 broadcast.366
  72.3 23.8 %scatter_fusion = bf16[384,8,128]{2,1,0:T(8,128)(2,1)} fusion(bf16[384,8,128]{2,1,0:T(8,128)(2,1)} %broadcast.366, s32[256]{0:T(256)S(1)} %bitcast.136, bf16[256,8,128]{2,1,0:T(8,128)(2,1)S(1)} %fusion.35), kind=kCustom, calls=%fused_computation.2 | custom fusion | bytes 1573888 | tf_op jit(solution)/shard_map/scatter | solution.py:127
  96.1 3.6 %all-to-all-start.1 = ((bf16[1,384,8,128]{3,2,0,1:T(8,128)(2,1)}), bf16[1,384,8,128]{3,2,0,1:T(8,128)(2,1)S(1)}, u32[]{:S(2)}, u32[]{:S(2)}) async-start(bf16[1,384,8,128]{3,2,0,1:T(8,128)(2,1)} %bitcast.40), calls=%async_computation.2 | async-start | bytes 1572864 | tf_op jit(solution)/shard_map/all_to_all | solution.py:129
  99.7 20.1 %psum.14 = f32[3,3,128]{2,0,1:T(4,128)S(1)} all-reduce(f32[3,3,128]{2,0,1:T(4,128)S(1)} %bitcast_add_fusion), channel_id=1, replica_groups=mesh['tile'=8,'chan'=4] {'tile'}, use_global_device_ids=true, to_apply=%region_17.18 | all-reduce | flops 1152 | bytes 9216 | tf_op jit(solution)/shard_map/psum | solution.py:134
  120.4 1.7 broadcast_multiply_fusion.9
  122.3 14.7 %scatter_fusion.1 = f32[256,8,128]{2,1,0:T(8,128)S(1)} fusion(f32[256,8,128]{2,1,0:T(8,128)S(1)} %broadcast.367, s32[384]{0:T(512)S(1)} %get-tuple-element.29, f32[384,8,128]{2,1,0:T(8,128)S(1)} %bitcast_convert_fusion), kind=kCustom, calls=%fused_computation.3 | custom fusion | flops 393216 | bytes 4720128 | tf_op jit(solution)/shard_map/scatter-add | solution.py:131
  137.9 21.8 %reduce-scatter.2.cloned.1.call-done = f32[1024,128]{1,0:T(8,128)} async-done(((f32[1024,512]{1,0:T(8,128)}), f32[1024,128]{1,0:T(8,128)}) %reduce-scatter.2.cloned.1.call-update) | async-done | bytes 524304 | tf_op jit(solution)/shard_map/reduce_scatter | solution.py:107
  159.7 1.8 %convert_bitcast_fusion.1 = bf16[1,1024,128]{2,1,0:T(8,128)(2,1)} fusion(f32[1024,128]{1,0:T(8,128)} %reduce-scatter.2.cloned.1.call-done), kind=kLoop, calls=%fused_computation.70 | loop fusion | flops 131072 | bytes 786432 | tf_op jit(solution)/shard_map/reshape | solution.py:108
  (60 shorter events, 9.5 us)
Async XLA Ops:
  7.2 3.3 %copy-start = (bf16[1,256,8,128]{3,2,1,0:T(8,128)(2,1)S(1)}, bf16[1,256,8,128]{3,2,1,0:T(8,128)(2,1)}, u32[]{:S(2)}) copy-start(bf16[1,256,8,128]{3,2,1,0:T(8,128)(2,1)} %param.9) | copy-start | bytes 1572868
  7.2 14.1 %copy-start.3 = (s32[8]{0:T(128)S(1)}, s32[8]{0:T(128)}, u32[]{:S(2)}) copy-start(s32[8]{0:T(128)} %param.13) | copy-start | bytes 100
  7.2 18.3 %copy-start.2 = (bf16[3,3,128]{2,1,0:T(4,128)(2,1)S(1)}, bf16[3,3,128]{2,1,0:T(4,128)(2,1)}, u32[]{:S(2)}) copy-start(bf16[3,3,128]{2,1,0:T(4,128)(2,1)} %param.15) | copy-start | bytes 6916
  15.4 17.8 %all-to-all-start = ((bf16[1,384,8,128]{3,2,0,1:T(8,128)(2,1)}), bf16[1,384,8,128]{3,2,0,1:T(8,128)(2,1)S(1)}, u32[]{:S(2)}, u32[]{:S(2)}) async-start(bf16[1,384,8,128]{3,2,0,1:T(8,128)(2,1)} %fusion.17), calls=%async_computation | async-start | bytes 1572864 | tf_op jit(solution)/shard_map/all_to_all | solution.py:94
  20.5 34.3 %all-gather.3.cloned.1.call-start = ((), (), s32[]{:S(2)}) async-start(), calls=%async_computation.5 | async-start | bytes 1310720 | tf_op jit(solution)/shard_map/all_gather | solution.py:110
  21.3 99.1 %all-reduce.11.cloned.1.call-start = ((), (), s32[]{:S(2)}) async-start(), calls=%async_computation.4 | async-start | bytes 524288 | tf_op jit(solution)/shard_map/psum | solution.py:134
  56.9 2.7 %copy-start.1 = (bf16[1,1024,512]{2,1,0:T(8,128)(2,1)S(1)}, bf16[1,1024,512]{2,1,0:T(8,128)(2,1)}, u32[]{:S(2)}) copy-start(bf16[1,1024,512]{2,1,0:T(8,128)(2,1)} %all-gather.3.cloned.1.call-done) | copy-start | bytes 3145732
  60.6 99.0 %reduce-scatter.2.cloned.1.call-start = ((), (), s32[]{:S(2)}) async-start(), calls=%async_computation.3 | async-start | bytes 2621440 | tf_op jit(solution)/shard_map/reduce_scatter | solution.py:107
  96.1 26.0 %all-to-all-start.1 = ((bf16[1,384,8,128]{3,2,0,1:T(8,128)(2,1)}), bf16[1,384,8,128]{3,2,0,1:T(8,128)(2,1)S(1)}, u32[]{:S(2)}, u32[]{:S(2)}) async-start(bf16[1,384,8,128]{3,2,0,1:T(8,128)(2,1)} %bitcast.40), calls=%async_computation.2 | async-start | bytes 1572864 | tf_op jit(solution)/shard_map/all_to_all | solution.py:129
Sparse Core Ops, SparseCore 0:
  22.9 31.8 all-gather.2
  60.8 52.7 all-reduce.10
  116.0 43.6 reduce-scatter.1
where the time goes:
time: 169 us; the launch traced here: 168 us
  waiting for transfers between devices  46.3 us (27%)
  other arithmetic  33.7 us (20%)
  local copies, waits for them, and re-layouts  31.5 us (19%)
  blocking collectives  20.1 us (12%)
  between operations  14.7 us (9%)
  matrix products  12.7 us (8%)
  starting transfers between devices  8.84 us (5%)
    scatter x1, local copies, waits for them, and re-layouts, body(): returning = returning.at[:, return_slot].set(grad_terms, mode='drop')  23.8 us
    reduce_scatter x1, waiting for transfers between devices, body(): lax.psum_scatter(partial_mix, 'chan', scatter_dimension=1, tiled=True)  21.8 us
    psum x1, blocking collectives, body(): kernel_sum, mix_sum = lax.psum((grad_kernel, grad_mix), 'tile')  20.1 us
    all_gather x1, waiting for transfers between devices, body(): piece = lax.all_gather(upstream, 'chan', axis=1, tiled=True)  16.9 us
    scatter-add x1, other arithmetic, body(): summed = summed.at[:, landing].add(arrived.astype(jnp.float32), mode='drop')  14.7 us
    all_to_all x1, waiting for transfers between devices, body(): lax.all_to_all(outgoing, 'tile', split_axis=1, concat_axis=1, tiled=True)  6.85 us
    all_to_all x1, starting transfers between devices, body(): lax.all_to_all(outgoing, 'tile', split_axis=1, concat_axis=1, tiled=True)  5.17 us
    dot_general x1, matrix products, body(): jnp.einsum('pk,bkc->bpc', weights, picked, preferred_element_type=jnp.flo...  3.93 us
  transfers between devices with their start and end apart: 5, of which 3 were waited for; matrix products, arithmetic and copies ran while one was open for 37% of the time, Pallas kernels for 0%

commit v1 on v0

--- a/solution.py
+++ b/solution.py
@@ -47,6 +47,13 @@
     return (jnp.stack(tap_rows), grad_field)
 
 
+def every_chan(block):
+    total = lax.axis_size("chan")
+    copies = jnp.broadcast_to(block[None], (total, *block.shape))
+    met = lax.all_to_all(copies, "chan", split_axis=0, concat_axis=0, tiled=True)
+    return jnp.concatenate([met[i] for i in range(total)], axis=1)
+
+
 def body(
     latlon,
     remap_weights,
@@ -70,15 +77,19 @@
     positions = jnp.arange(terms_max, dtype=jnp.int32)
     in_use = positions[None, :] < term_count[:, None]
     mine = in_use & (term_source == tile_now)
-    send_rank = jnp.cumsum(mine.astype(jnp.int32), axis=1) - 1
+    before = (positions[:, None] <= positions[None, :]).astype(jnp.bfloat16)
+    send_rank = jnp.dot(mine.astype(jnp.bfloat16), before, preferred_element_type=jnp.float32)
+    send_rank = send_rank.astype(jnp.int32) - 1
     slot_ids = jnp.arange(capacity, dtype=jnp.int32)
-    slot_hits = mine[:, :, None] & (send_rank[:, :, None] == slot_ids[None, None, :])
-    slot_filled = jnp.any(slot_hits, axis=1).reshape(-1)
-    slot_block = jnp.sum(jnp.where(slot_hits, term_block[:, :, None], 0), axis=1).reshape(-1)
-    outgoing = jnp.take(latlon, slot_block, axis=1)
-    outgoing = jnp.where(slot_filled[None, :, None, None], outgoing, jnp.zeros((), latlon.dtype))
-    own_source = lax.dynamic_index_in_dim(term_source, tile_now, 0, keepdims=False)
-    own_count = lax.dynamic_index_in_dim(term_count, tile_now, 0, keepdims=False)
+    slot_hits = mine[:, None, :] & (send_rank[:, None, :] == slot_ids[None, :, None])
+    slot_block = (jnp.sum(jnp.where(slot_hits, term_block[:, None, :] + 1, 0), axis=2) - 1).reshape(-1)
+    blocks = jnp.arange(block_total, dtype=jnp.int32)
+    send_pick = (slot_block[:, None] == blocks[None, :]).astype(jnp.bfloat16)
+    outgoing = jnp.einsum("nb,abkc->ankc", send_pick, latlon, preferred_element_type=jnp.float32)
+    outgoing = outgoing.astype(jnp.bfloat16)
+    tile_mask = (jnp.arange(tile_total) == tile_now)[:, None]
+    own_source = jnp.sum(jnp.where(tile_mask, term_source, 0), axis=0)
+    own_count = jnp.sum(jnp.where(tile_mask[:, 0], term_count, 0))
     own_use = positions < own_count
     same_source = (
         (own_source[None, :] == own_source[:, None])
@@ -86,14 +97,15 @@
         & (positions[None, :] <= positions[:, None])
     )
     own_rank = jnp.sum(same_source.astype(jnp.int32), axis=1) - 1
-    recv_slot = jnp.where(own_use, own_source * capacity + own_rank, 0)
-    return_slot = jnp.where(own_use, own_source * capacity + own_rank, tile_total * capacity)
+    recv_slot = jnp.where(own_use, own_source * capacity + own_rank, -1)
+    slots = jnp.arange(tile_total * capacity, dtype=jnp.int32)
+    recv_pick = (recv_slot[:, None] == slots[None, :]).astype(jnp.bfloat16)
     weights = remap_weights[0]
     ext_cells = weights.shape[0]
     term_pts = weights.shape[1]
     arrived = lax.all_to_all(outgoing, "tile", split_axis=1, concat_axis=1, tiled=True)
-    picked = jnp.take(arrived, recv_slot, axis=1)
-    picked = jnp.where(own_use[None, :, None, None], picked, jnp.zeros((), arrived.dtype))
+    picked = jnp.einsum("tn,ankc->atkc", recv_pick, arrived, preferred_element_type=jnp.float32)
+    picked = picked.astype(jnp.bfloat16)
     picked = picked.reshape(picked.shape[0], term_pts, chan_local)
     mapped = jnp.einsum("pk,bkc->bpc", weights, picked, preferred_element_type=jnp.float32)
     remapped = mapped.astype(jnp.bfloat16)
@@ -103,11 +115,11 @@
     hidden = stencil_apply(field, kernel)
     active = jax.nn.silu(hidden).astype(jnp.bfloat16).reshape(flat_rows, chan_local)
     own_rows = lax.dynamic_slice_in_dim(pointwise, chan_now * chan_local, chan_local, 0)
-    partial_mix = jnp.dot(active, own_rows, preferred_element_type=jnp.float32)
-    mixed = lax.psum_scatter(partial_mix, "chan", scatter_dimension=1, tiled=True)
+    own_cols = lax.dynamic_slice_in_dim(pointwise, chan_now * chan_local, chan_local, 1)
+    mixed = jnp.dot(every_chan(active), own_cols, preferred_element_type=jnp.float32)
     coupled = mixed.astype(jnp.bfloat16).reshape(batch_rows, tile_cells, chan_local)
     upstream = cotangent.reshape(flat_rows, chan_local)
-    piece = lax.all_gather(upstream, "chan", axis=1, tiled=True)
+    piece = every_chan(upstream)
     grad_active = lax.dot_general(
         piece, own_rows, (((1,), (1,)), ((), ())), preferred_element_type=jnp.float32
     )
@@ -121,14 +133,11 @@
     grad_turned, grad_field = stencil_grads(field, kernel, grad_hidden)
     grad_field = grad_field.astype(jnp.bfloat16).reshape(batch_rows, ext_cells, chan_local)
     grad_terms = jnp.einsum("pk,bpc->bkc", weights, grad_field, preferred_element_type=jnp.float32)
-    grad_terms = grad_terms.reshape(batch_rows, terms_max, seg_len, chan_local)
-    grad_terms = jnp.where(own_use[None, :, None, None], grad_terms, 0.0).astype(jnp.bfloat16)
-    returning = jnp.zeros((batch_rows, tile_total * capacity, seg_len, chan_local), jnp.bfloat16)
-    returning = returning.at[:, return_slot].set(grad_terms, mode="drop")
-    landing = jnp.where(slot_filled, slot_block, block_total)
+    grad_terms = grad_terms.astype(jnp.bfloat16).reshape(batch_rows, terms_max, seg_len, chan_local)
+    returning = jnp.einsum("tn,atkc->ankc", recv_pick, grad_terms, preferred_element_type=jnp.float32)
+    returning = returning.astype(jnp.bfloat16)
     arrived = lax.all_to_all(returning, "tile", split_axis=1, concat_axis=1, tiled=True)
-    summed = jnp.zeros((arrived.shape[0], block_total, seg_len, chan_local), jnp.float32)
-    summed = summed.at[:, landing].add(arrived.astype(jnp.float32), mode="drop")
+    summed = jnp.einsum("nb,ankc->abkc", send_pick, arrived, preferred_element_type=jnp.float32)
     grad_latlon = summed.astype(jnp.bfloat16)
     grad_kernel = turn_kernel(grad_turned, turn, -1)
     kernel_sum, mix_sum = lax.psum((grad_kernel, grad_mix), "tile")

time: 169 us -> 159 us (0.941)
  other arithmetic: 33.7 us -> 8.01 us
  local copies, waits for them, and re-layouts: 31.5 us -> 9.13 us
  waiting for transfers between devices: 46.3 us -> 67.7 us
  blocking collectives: 20.1 us -> 29.7 us
  starting transfers between devices: 8.84 us -> 13.6 us
  matrix products: 12.7 us -> 15.6 us
    psum x1, waiting for transfers between devices: 0.01 us -> 42.3 us  [body(): kernel_sum, mix_sum = lax.psum((grad_kernel, grad_mix), 'tile')]
    scatter x1 -> x0, local copies, waits for them, and re-layouts: 23.8 us -> none  [body(): returning = returning.at[:, return_slot].set(grad_terms, mode='drop')]
    reduce_scatter x1 -> x0, waiting for transfers between devices: 21.8 us -> none  [body(): lax.psum_scatter(partial_mix, 'chan', scatter_dimension=1, tiled=True)]
    all_to_all x0 -> x1, blocking collectives: none -> 17.2 us  [body(): lax.all_to_all(returning, 'tile', split_axis=1, concat_axis=1, tiled=True)]
    all_gather x1 -> x0, waiting for transfers between devices: 16.9 us -> none  [body(): piece = lax.all_gather(upstream, 'chan', axis=1, tiled=True)]
    all_to_all x1 -> x2, waiting for transfers between devices: 0.01 us -> 15.1 us  [every_chan(): lax.all_to_all(copies, 'chan', split_axis=0, concat_axis=0, tiled=True)]
    scatter-add x1 -> x0, other arithmetic: 14.7 us -> none  [body(): summed = summed.at[:, landing].add(arrived.astype(jnp.float32), mode='drop')]
    psum x1, blocking collectives: 20.1 us -> 12.5 us  [body(): kernel_sum, mix_sum = lax.psum((grad_kernel, grad_mix), 'tile')]
  transfers between devices with their start and end apart: 5 -> 4, of which waited for: 3 -> 3; matrix products, arithmetic and copies ran while one was open for 37% -> 10% of each run, Pallas kernels for 0% -> 0%
where the time goes in v1:
time: 159 us
  waiting for transfers between devices  67.7 us (43%)
  blocking collectives  29.7 us (19%)
  matrix products  15.6 us (10%)
  between operations  15 us (9%)
  starting transfers between devices  13.6 us (9%)
  local copies, waits for them, and re-layouts  9.13 us (6%)
  other arithmetic  8.01 us (5%)
    psum x1, waiting for transfers between devices, body(): kernel_sum, mix_sum = lax.psum((grad_kernel, grad_mix), 'tile')  42.3 us
    all_to_all x1, blocking collectives, body(): lax.all_to_all(returning, 'tile', split_axis=1, concat_axis=1, tiled=True)  17.2 us
    all_to_all x2, waiting for transfers between devices, every_chan(): lax.all_to_all(copies, 'chan', split_axis=0, concat_axis=0, tiled=True)  15.1 us
    psum x1, blocking collectives, body(): kernel_sum, mix_sum = lax.psum((grad_kernel, grad_mix), 'tile')  12.5 us
    all_to_all x1, waiting for transfers between devices, body(): lax.all_to_all(outgoing, 'tile', split_axis=1, concat_axis=1, tiled=True)  10.3 us
    all_to_all x2, starting transfers between devices, every_chan(): lax.all_to_all(copies, 'chan', split_axis=0, concat_axis=0, tiled=True)  8.39 us
    all_to_all x1, starting transfers between devices, body(): lax.all_to_all(outgoing, 'tile', split_axis=1, concat_axis=1, tiled=True)  5.17 us
    dot_general x1, matrix products, body(): jnp.einsum('pk,bkc->bpc', weights, picked, preferred_element_type=jnp.flo...  3.74 us
  transfers between devices with their start and end apart: 4, of which 3 were waited for; matrix products, arithmetic and copies ran while one was open for 10% of the time, Pallas kernels for 0%

profile of v1, /device:TPU:0, one launch (start us, length us, event | category | flops | bytes accessed | tf_op | source)
XLA Modules:
  0.0 158.7 jit_solution(14741174235039871725)
XLA Ops:
  7.2 0.8 fusion.67
  8.2 0.7 broadcast_add_fusion
  9.7 1.4 copy.70
  11.1 5.2 %all-to-all-start = ((bf16[1,384,8,128]{3,2,0,1:T(8,128)(2,1)}), bf16[1,384,8,128]{3,2,0,1:T(8,128)(2,1)S(1)}, u32[]{:S(2)}, u32[]{:S(2)}) async-start(bf16[1,384,8,128]{3,2,0,1:T(8,128)(2,1)} %copy.70), calls=%async_computation | async-start | bytes 1572864 | tf_op jit(solution)/shard_map/all_to_all | solution.py:106
  18.5 10.3 %all-to-all-done = bf16[1,384,8,128]{3,2,0,1:T(8,128)(2,1)S(1)} async-done(((bf16[1,384,8,128]{3,2,0,1:T(8,128)(2,1)}), bf16[1,384,8,128]{3,2,0,1:T(8,128)(2,1)S(1)}, u32[]{:S(2)}, u32[]{:S(2)}) %all-to-all-start) | async-done | bytes 786464 | tf_op jit(solution)/shard_map/all_to_all | solution.py:106
  28.8 1.1 broadcast_in_dim.81
  30.0 4.9 %all-to-all-start.2 = ((bf16[4,1024,128]{2,1,0:T(8,128)(2,1)}), bf16[4,1024,128]{2,1,0:T(8,128)(2,1)S(1)}, u32[]{:S(2)}, u32[]{:S(2)}) async-start(bf16[4,1024,128]{2,1,0:T(8,128)(2,1)} %broadcast_in_dim.81), calls=%async_computation.2 | async-start | bytes 2097152 | tf_op jit(solution)/shard_map/all_to_all | solution.py:53
  36.1 1.3 fusion.18
  37.4 1.4 copy.72
  38.8 3.7 %fusion.13 = bf16[1,1156,128]{2,1,0:T(8,128)(2,1)S(1)} fusion(bf16[1,1156,2048]{2,1,0:T(8,128)(2,1)} %param.10, bf16[1,256,8,128]{3,2,1,0:T(8,128)(2,1)S(1)} %copy.72), kind=kOutput, calls=%fused_computation.7 | convolution fusion | flops 606224896 | bytes 5555200 | tf_op jit(solution)/shard_map/pk,bkc->bpc/dot_general | solution.py:110
  42.6 15.1 %all-to-all-done.2 = bf16[4,1024,128]{2,1,0:T(8,128)(2,1)S(1)} async-done(((bf16[4,1024,128]{2,1,0:T(8,128)(2,1)}), bf16[4,1024,128]{2,1,0:T(8,128)(2,1)S(1)}, u32[]{:S(2)}, u32[]{:S(2)}) %all-to-all-start.2) | async-done | bytes 1048608 | tf_op jit(solution)/shard_map/all_to_all | solution.py:53
  57.9 1.5 fusion.64
  59.4 0.9 fusion.39
  61.0 0.7 add_convert_fusion
  61.8 3.3 %fusion.10 = bf16[1,2048,128]{1,2,0:T(8,128)(2,1)S(1)} fusion(bf16[1156,128]{1,0:T(8,128)(2,1)S(1)} %reshape.130, bf16[1,1156,2048]{2,1,0:T(8,128)(2,1)} %param.10), kind=kOutput, calls=%fused_computation.6 | convolution fusion | flops 606339072 | bytes 5555200 | tf_op jit(solution)/shard_map/pk,bpc->bkc/dot_general | solution.py:135
  66.5 17.2 %all_to_all.20 = bf16[1,384,8,128]{3,2,0,1:T(8,128)(2,1)S(1)} all-to-all(bf16[1,384,8,128]{3,2,0,1:T(8,128)(2,1)S(1)} %copy.75), channel_id=1, replica_groups=mesh['tile'=8,'chan'=4] {'tile'}, dimensions={1} | all-to-all | bytes 1572864 | tf_op jit(solution)/shard_map/all_to_all | solution.py:139
  83.6 1.1 broadcast_in_dim.79
  84.8 3.5 %all-to-all-start.1 = ((bf16[4,1024,128]{2,1,0:T(8,128)(2,1)}), bf16[4,1024,128]{2,1,0:T(8,128)(2,1)S(1)}, u32[]{:S(2)}, u32[]{:S(2)}) async-start(bf16[4,1024,128]{2,1,0:T(8,128)(2,1)} %broadcast_in_dim.79), calls=%async_computation.1 | async-start | bytes 2097152 | tf_op jit(solution)/shard_map/all_to_all | solution.py:53
  88.5 2.0 %fusion.63 = f32[128,512]{1,0:T(8,128)} fusion(bf16[1024,128]{1,0:T(8,128)(2,1)S(1)} %bitcast.135, bf16[1024,128]{1,0:T(8,128)(2,1)S(1)} %copy-done.3, bf16[1024,128]{1,0:T(8,128)(2,1)S(1)} %copy-done.5, bf16[1024,128]{1,0:T(8,128)(2,1)} %copy-done.6, bf16[1024,128]{1,0:T(8,128)(2,1)S(1)} %get-tuple-element.35), kind=kOutput, calls=%fused_computation.104 | convolution fusion | flops 138412032 | bytes 1572864 | tf_op jit(solution)/shard_map/dot_general | solution.py:126
  90.5 12.5 %psum.14 = f32[3,3,128]{2,0,1:T(4,128)S(1)} all-reduce(f32[3,3,128]{2,0,1:T(4,128)S(1)} %bitcast_add_fusion), channel_id=1, replica_groups=mesh['tile'=8,'chan'=4] {'tile'}, use_global_device_ids=true, to_apply=%region_13.14 | all-reduce | flops 1152 | bytes 9216 | tf_op jit(solution)/shard_map/psum | solution.py:143
  103.6 42.3 %all-reduce.11.cloned.1.call-done = f32[128,512]{1,0:T(8,128)} async-done(((f32[128,512]{1,0:T(8,128)}), f32[128,512]{1,0:T(8,128)}) %all-reduce.11.cloned.1.call-update) | async-done | bytes 262160 | tf_op jit(solution)/shard_map/psum | solution.py:143
  145.9 1.7 %broadcast_multiply_fusion.9 = f32[128,512]{1,0:T(8,128)} fusion(f32[128,512]{1,0:T(8,128)} %all-reduce.11.cloned.1.call-done), kind=kLoop, calls=%fused_computation.106 | loop fusion | flops 65536 | bytes 524288 | tf_op jit(solution)/shard_map/mul | solution.py:145
  148.6 1.1 copy.83
  149.8 2.1 %fusion.20 = bf16[1,1024,128]{2,1,0:T(8,128)(2,1)} fusion(bf16[1024,128]{1,0:T(8,128)(2,1)S(1)} %get-tuple-element.32, bf16[1024,128]{1,0:T(8,128)(2,1)S(1)} %get-tuple-element.33, bf16[1024,128]{1,0:T(8,128)(2,1)S(1)} %get-tuple-element.34, bf16[1024,128]{1,0:T(8,128)(2,1)S(1)} %get-tuple-element.31, bf16[512,512]{1,0:T(8,128)(2,1)} %param.16, ...), kind=kOutput, calls=%fused_computation.17 | convolution fusion | flops 138543104 | bytes 1441796 | tf_op jit(solution)/shard_map/dot_general | solution.py:119
  (60 shorter events, 7.9 us)
Async XLA Ops:
  7.2 2.0 %copy-start = (bf16[1,256,8,128]{3,2,1,0:T(8,128)(2,1)S(1)}, bf16[1,256,8,128]{3,2,1,0:T(8,128)(2,1)}, u32[]{:S(2)}) copy-start(bf16[1,256,8,128]{3,2,1,0:T(8,128)(2,1)} %param.9) | copy-start | bytes 1572868
  9.2 7.0 %copy-start.8 = (bf16[3,3,128]{2,1,0:T(4,128)(2,1)S(1)}, bf16[3,3,128]{2,1,0:T(4,128)(2,1)}, u32[]{:S(2)}) copy-start(bf16[3,3,128]{2,1,0:T(4,128)(2,1)} %param.15) | copy-start | bytes 6916
  9.2 7.8 %copy-start.9 = (s32[8]{0:T(128)S(1)}, s32[8]{0:T(128)}, u32[]{:S(2)}) copy-start(s32[8]{0:T(128)} %param.13) | copy-start | bytes 100
  9.2 9.0 %copy-start.7 = (s32[8,256]{1,0:T(8,128)S(1)}, s32[8,256]{1,0:T(8,128)}, u32[]{:S(2)}) copy-start(s32[8,256]{1,0:T(8,128)} %param.11) | copy-start | bytes 24580
  9.2 19.6 %copy-start.1 = (bf16[1,1024,128]{2,1,0:T(8,128)(2,1)S(1)}, bf16[1,1024,128]{2,1,0:T(8,128)(2,1)}, u32[]{:S(2)}) copy-start(bf16[1,1024,128]{2,1,0:T(8,128)(2,1)} %param.17) | copy-start | bytes 786436
  11.1 17.8 %all-to-all-start = ((bf16[1,384,8,128]{3,2,0,1:T(8,128)(2,1)}), bf16[1,384,8,128]{3,2,0,1:T(8,128)(2,1)S(1)}, u32[]{:S(2)}, u32[]{:S(2)}) async-start(bf16[1,384,8,128]{3,2,0,1:T(8,128)(2,1)} %copy.70), calls=%async_computation | async-start | bytes 1572864 | tf_op jit(solution)/shard_map/all_to_all | solution.py:106
  30.0 27.8 %all-to-all-start.2 = ((bf16[4,1024,128]{2,1,0:T(8,128)(2,1)}), bf16[4,1024,128]{2,1,0:T(8,128)(2,1)S(1)}, u32[]{:S(2)}, u32[]{:S(2)}) async-start(bf16[4,1024,128]{2,1,0:T(8,128)(2,1)} %broadcast_in_dim.81), calls=%async_computation.2 | async-start | bytes 2097152 | tf_op jit(solution)/shard_map/all_to_all | solution.py:53
  57.8 2.5 %copy-start.2 = (bf16[1024,128]{1,0:T(8,128)(2,1)}, bf16[1024,128]{1,0:T(8,128)(2,1)S(1)}, u32[]{:S(2)}) copy-start(bf16[1024,128]{1,0:T(8,128)(2,1)S(1)} %get-tuple-element.36) | copy-start | bytes 786436
  57.8 2.5 %copy-start.4 = (bf16[1024,128]{1,0:T(8,128)(2,1)}, bf16[1024,128]{1,0:T(8,128)(2,1)S(1)}, u32[]{:S(2)}) copy-start(bf16[1024,128]{1,0:T(8,128)(2,1)S(1)} %get-tuple-element.37) | copy-start | bytes 786436
  57.9 3.1 %copy-start.6 = (bf16[1024,128]{1,0:T(8,128)(2,1)}, bf16[1024,128]{1,0:T(8,128)(2,1)S(1)}, u32[]{:S(2)}) copy-start(bf16[1024,128]{1,0:T(8,128)(2,1)S(1)} %get-tuple-element.38) | copy-start | bytes 786436
  83.6 4.8 %copy-start.3 = (bf16[1024,128]{1,0:T(8,128)(2,1)S(1)}, bf16[1024,128]{1,0:T(8,128)(2,1)}, u32[]{:S(2)}) copy-start(bf16[1024,128]{1,0:T(8,128)(2,1)} %copy-done.2) | copy-start | bytes 786436
  83.6 4.8 %copy-start.5 = (bf16[1024,128]{1,0:T(8,128)(2,1)S(1)}, bf16[1024,128]{1,0:T(8,128)(2,1)}, u32[]{:S(2)}) copy-start(bf16[1024,128]{1,0:T(8,128)(2,1)} %copy-done.4) | copy-start | bytes 786436
  84.8 64.9 %all-to-all-start.1 = ((bf16[4,1024,128]{2,1,0:T(8,128)(2,1)}), bf16[4,1024,128]{2,1,0:T(8,128)(2,1)S(1)}, u32[]{:S(2)}, u32[]{:S(2)}) async-start(bf16[4,1024,128]{2,1,0:T(8,128)(2,1)} %broadcast_in_dim.79), calls=%async_computation.1 | async-start | bytes 2097152 | tf_op jit(solution)/shard_map/all_to_all | solution.py:53
  88.3 57.6 %all-reduce.11.cloned.1.call-start = ((), (), s32[]{:S(2)}) async-start(), calls=%async_computation.4 | async-start | bytes 524288 | tf_op jit(solution)/shard_map/psum | solution.py:143
Sparse Core Ops, SparseCore 0:
  92.8 53.0 all-reduce.10

commit v2 on v1

--- a/solution.py
+++ b/solution.py
@@ -3,6 +3,8 @@
 import jax
 import jax.numpy as jnp
 from jax import lax
+from jax.experimental import pallas as pl
+from jax.experimental.pallas import tpu as pltpu
 from jax.sharding import PartitionSpec as P
 
 TILE_EDGE = 32
@@ -47,11 +49,190 @@
     return (jnp.stack(tap_rows), grad_field)
 
 
-def every_chan(block):
-    total = lax.axis_size("chan")
-    copies = jnp.broadcast_to(block[None], (total, *block.shape))
-    met = lax.all_to_all(copies, "chan", split_axis=0, concat_axis=0, tiled=True)
-    return jnp.concatenate([met[i] for i in range(total)], axis=1)
+CHUNKS = 4
+
+
+def greet():
+    barrier = pltpu.get_barrier_semaphore()
+    met = 0
+    for axis in ("tile", "chan"):
+        total, here = lax.axis_size(axis), lax.axis_index(axis)
+        for step in range(1, total):
+            pl.semaphore_signal(
+                barrier,
+                inc=1,
+                device_id={axis: lax.rem(here + step, total)},
+                device_id_type=pl.DeviceIdType.MESH,
+            )
+            met += 1
+    pl.semaphore_wait(barrier, met)
+
+
+def send(src, dst, sems, place, where):
+    copy = pltpu.make_async_remote_copy(
+        src_ref=src,
+        dst_ref=dst,
+        send_sem=sems.at[(0, *place)],
+        recv_sem=sems.at[(1, *place)],
+        device_id=where,
+        device_id_type=pl.DeviceIdType.MESH,
+    )
+    return copy
+
+
+def swap_start(src, dst, rows, sems, spread):
+    total, here = lax.axis_size("tile"), lax.axis_index("tile")
+    into = pl.ds(pl.multiple_of(here * rows, rows), rows)
+    own = src if spread else src.at[into]
+    copies = [pltpu.make_async_copy(own, dst.at[into], sems.at[0, 0])]
+    for step in range(1, total):
+        peer = lax.rem(here + step, total)
+        part = src if spread else src.at[pl.ds(pl.multiple_of(peer * rows, rows), rows)]
+        copies.append(send(part, dst.at[into], sems, (step,), {"tile": peer}))
+    for copy in copies:
+        copy.start()
+    return copies
+
+
+def wait_all(copies):
+    for copy in copies:
+        copy.wait()
+
+
+def line_gather(own, full, sems, local_sem, after=None):
+    total, here = lax.axis_size("chan"), lax.axis_index("chan")
+    wide, rows = own.shape[1], own.shape[0] // CHUNKS
+
+    def at(ref, who, chunk):
+        return ref.at[
+            pl.ds(chunk * rows, rows), pl.ds(pl.multiple_of(who * wide, wide), wide)
+        ]
+
+    def hop(way, step, chunk):
+        shift = 1 - 2 * way
+        who = jnp.clip(here - shift * step, 0, total - 1)
+        src = own.at[pl.ds(chunk * rows, rows)] if step == 0 else at(full, who, chunk)
+        return send(
+            src,
+            at(full, who, chunk),
+            sems,
+            (way, step, chunk),
+            {"chan": jnp.clip(here + shift, 0, total - 1)},
+        )
+
+    def far(way, step):
+        return here >= step if way == 0 else here <= total - 1 - step
+
+    def sends(way, step):
+        return far(way, step) & (here < total - 1 if way == 0 else here > 0)
+
+    local = pltpu.make_async_copy(
+        own, full.at[:, pl.ds(pl.multiple_of(here * wide, wide), wide)], local_sem
+    )
+    local.start()
+    for step in range(total):
+        for chunk in range(CHUNKS):
+            for way in range(2):
+                if step > 0:
+
+                    @pl.when(far(way, step))
+                    def _(way=way, step=step, chunk=chunk):
+                        hop(way, step - 1, chunk).wait_recv()
+
+                if step < total - 1:
+
+                    @pl.when(sends(way, step))
+                    def _(way=way, step=step, chunk=chunk):
+                        hop(way, step, chunk).start()
+
+        if step == 1 and after is not None:
+            after()
+    for step in range(total - 1):
+        for chunk in range(CHUNKS):
+            for way in range(2):
+
+                @pl.when(sends(way, step))
+                def _(way=way, step=step, chunk=chunk):
+                    hop(way, step, chunk).wait_send()
+
+    local.wait()
+
+
+def first_kernel(out_ref, own_ref, in_ref, full_ref, swap_sems, line_sems, local_sem):
+    greet()
+    rows = out_ref.shape[0] // lax.axis_size("tile")
+    copies = swap_start(out_ref, in_ref, rows, swap_sems, False)
+    line_gather(own_ref, full_ref, line_sems, local_sem)
+    wait_all(copies)
+
+
+def second_kernel(
+    out_ref,
+    own_ref,
+    mix_ref,
+    taps_ref,
+    in_ref,
+    full_ref,
+    mix_out,
+    taps_out,
+    mix_parts,
+    mix_own,
+    taps_parts,
+    swap_sems,
+    line_sems,
+    mix_sems,
+    back_sems,
+    taps_sems,
+    local_sem,
+):
+    greet()
+    total = lax.axis_size("tile")
+    mix_rows = mix_ref.shape[0] // total
+    mix_copies = swap_start(mix_ref, mix_parts, mix_rows, mix_sems, False)
+    taps_copies = swap_start(taps_ref, taps_parts, taps_ref.shape[0], taps_sems, True)
+    copies = swap_start(out_ref, in_ref, out_ref.shape[0] // total, swap_sems, False)
+    back = []
+
+    def reduce():
+        wait_all(mix_copies)
+        summed = mix_parts[0:mix_rows]
+        for part in range(1, total):
+            summed = summed + mix_parts[part * mix_rows : (part + 1) * mix_rows]
+        mix_own[...] = summed.astype(mix_own.dtype)
+        back.extend(swap_start(mix_own, mix_out, mix_rows, back_sems, True))
+
+    line_gather(own_ref, full_ref, line_sems, local_sem, reduce)
+    wait_all(taps_copies)
+    tap_rows = taps_ref.shape[0]
+    taps = taps_parts[0:tap_rows]
+    for part in range(1, total):
+        taps = taps + taps_parts[part * tap_rows : (part + 1) * tap_rows]
+    taps_out[...] = taps
+    wait_all(back)
+    wait_all(copies)
+
+
+def call(kernel, shapes, scratch, sems, collective_id, *operands):
+    vmem = pl.BlockSpec(memory_space=pltpu.VMEM)
+    line = (2, 2, lax.axis_size("chan"), CHUNKS)
+    return pl.pallas_call(
+        kernel,
+        out_shape=[jax.ShapeDtypeStruct(*one) for one in shapes],
+        in_specs=[vmem] * len(operands),
+        out_specs=[vmem] * len(shapes),
+        scratch_shapes=[
+            *[pltpu.VMEM(*one) for one in scratch],
+            pltpu.SemaphoreType.DMA((2, lax.axis_size("tile"))),
+            pltpu.SemaphoreType.DMA(line),
+            *[pltpu.SemaphoreType.DMA((2, lax.axis_size("tile")))] * sems,
+            pltpu.SemaphoreType.DMA,
+        ],
+        compiler_params=pltpu.CompilerParams(
+            collective_id=collective_id,
+            has_side_effects=True,
+            vmem_limit_bytes=24 * 2**20,
+        ),
+    )(*operands)
 
 
 def body(
@@ -103,7 +284,21 @@
     weights = remap_weights[0]
     ext_cells = weights.shape[0]
     term_pts = weights.shape[1]
-    arrived = lax.all_to_all(outgoing, "tile", split_axis=1, concat_axis=1, tiled=True)
+    slot_shape = outgoing.shape
+    upstream = cotangent.reshape(flat_rows, chan_local)
+    chan_total = lax.axis_size("chan")
+    outgoing = outgoing.reshape(-1, chan_local)
+    whole_shape = (flat_rows, chan_total * chan_local)
+    arrived, piece = call(
+        first_kernel,
+        ((outgoing.shape, jnp.bfloat16), (whole_shape, jnp.bfloat16)),
+        (),
+        0,
+        0,
+        outgoing,
+        upstream,
+    )
+    arrived = arrived.reshape(slot_shape)
     picked = jnp.einsum("tn,ankc->atkc", recv_pick, arrived, preferred_element_type=jnp.float32)
     picked = picked.astype(jnp.bfloat16)
     picked = picked.reshape(picked.shape[0], term_pts, chan_local)
@@ -116,10 +311,6 @@
     active = jax.nn.silu(hidden).astype(jnp.bfloat16).reshape(flat_rows, chan_local)
     own_rows = lax.dynamic_slice_in_dim(pointwise, chan_now * chan_local, chan_local, 0)
     own_cols = lax.dynamic_slice_in_dim(pointwise, chan_now * chan_local, chan_local, 1)
-    mixed = jnp.dot(every_chan(active), own_cols, preferred_element_type=jnp.float32)
-    coupled = mixed.astype(jnp.bfloat16).reshape(batch_rows, tile_cells, chan_local)
-    upstream = cotangent.reshape(flat_rows, chan_local)
-    piece = every_chan(upstream)
     grad_active = lax.dot_general(
         piece, own_rows, (((1,), (1,)), ((), ())), preferred_element_type=jnp.float32
     )
@@ -136,11 +327,44 @@
     grad_terms = grad_terms.astype(jnp.bfloat16).reshape(batch_rows, terms_max, seg_len, chan_local)
     returning = jnp.einsum("tn,atkc->ankc", recv_pick, grad_terms, preferred_element_type=jnp.float32)
     returning = returning.astype(jnp.bfloat16)
-    arrived = lax.all_to_all(returning, "tile", split_axis=1, concat_axis=1, tiled=True)
+    grad_kernel = turn_kernel(grad_turned, turn, -1).reshape(9, chan_local)
+    grad_kernel = jnp.pad(grad_kernel, ((0, 7), (0, 0)))
+    grad_mix = jnp.concatenate(
+        [grad_mix[:, i * chan_local : (i + 1) * chan_local] for i in range(chan_total)]
+    )
+    returning = returning.reshape(-1, chan_local)
+    mix_rows = grad_mix.shape[0] // tile_total
+    mix_type = jnp.bfloat16 if mix_rows % 16 == 0 else jnp.float32
+    arrived, active_all, mix_sum, kernel_sum = call(
+        second_kernel,
+        (
+            (returning.shape, jnp.bfloat16),
+            (whole_shape, jnp.bfloat16),
+            (grad_mix.shape, mix_type),
+            (grad_kernel.shape, jnp.float32),
+        ),
+        (
+            (grad_mix.shape, jnp.float32),
+            ((mix_rows, chan_local), mix_type),
+            ((tile_total * grad_kernel.shape[0], chan_local), jnp.float32),
+        ),
+        3,
+        1,
+        returning,
+        active,
+        grad_mix,
+        grad_kernel,
+    )
+    mixed = jnp.dot(active_all, own_cols, preferred_element_type=jnp.float32)
+    coupled = mixed.astype(jnp.bfloat16).reshape(batch_rows, tile_cells, chan_local)
+    arrived = arrived.reshape(slot_shape)
+    mix_sum = mix_sum.astype(jnp.float32)
+    mix_sum = jnp.concatenate(
+        [mix_sum[i * chan_local : (i + 1) * chan_local] for i in range(chan_total)], axis=1
+    )
+    kernel_sum = kernel_sum[:9].reshape(3, 3, chan_local)
     summed = jnp.einsum("nb,ankc->abkc", send_pick, arrived, preferred_element_type=jnp.float32)
     grad_latlon = summed.astype(jnp.bfloat16)
-    grad_kernel = turn_kernel(grad_turned, turn, -1)
-    kernel_sum, mix_sum = lax.psum((grad_kernel, grad_mix), "tile")
     factor = 1.0 / math.sqrt(batch_rows * tile_cells * tile_total)
     return (coupled, grad_latlon, kernel_sum * factor, mix_sum * factor)
 

time: 159 us -> 77 us (0.48)
  waiting for transfers between devices: 67.7 us -> 0 us
  Pallas kernels: 0 us -> 46.1 us
  blocking collectives: 29.7 us -> 0 us
  starting transfers between devices: 13.6 us -> 0 us
  between operations: 15 us -> 1.56 us
  local copies, waits for them, and re-layouts: 9.13 us -> 6.45 us
  matrix products: 15.6 us -> 14 us
    pallas_call x0 -> x2, Pallas kernels: none -> 46.1 us  [call(): pl.pallas_call(kernel, out_shape=[jax.ShapeDtypeStruct(*one) for one in s...]
    psum x1 -> x0, waiting for transfers between devices: 42.3 us -> none  [body(): kernel_sum, mix_sum = lax.psum((grad_kernel, grad_mix), 'tile')]
    all_to_all x3 -> x0, waiting for transfers between devices: 25.4 us -> none  [the longest x2 15.1 us: every_chan(): lax.all_to_all(copies, 'chan', split_axis=0, concat_axis=0, tiled=True)]
    all_to_all x1 -> x0, blocking collectives: 17.2 us -> none  [body(): lax.all_to_all(returning, 'tile', split_axis=1, concat_axis=1, tiled=True)]
    all_to_all x3 -> x0, starting transfers between devices: 13.6 us -> none  [the longest x2 8.39 us: every_chan(): lax.all_to_all(copies, 'chan', split_axis=0, concat_axis=0, tiled=True)]
    psum x1 -> x0, blocking collectives: 12.5 us -> none  [body(): kernel_sum, mix_sum = lax.psum((grad_kernel, grad_mix), 'tile')]
    broadcast_in_dim x2 -> x0, local copies, waits for them, and re-layouts: 2.25 us -> none  [every_chan(): copies = jnp.broadcast_to(block[None], (total, *block.shape))]
    dot_general x1, matrix products: 1.99 us -> 0.33 us  [body(): lax.dot_general(active, piece, (((0,), (0,)), ((), ())), preferred_elemen...]
  transfers between devices with their start and end apart: 4 -> 0, of which waited for: 3 -> 0; matrix products, arithmetic and copies ran while one was open for 10% -> 0% of each run, Pallas kernels for 0% -> 0%
where the time goes in v2:
time: 77 us; the launch traced here: 76.5 us
  Pallas kernels  46.1 us (60%)
  matrix products  14 us (18%)
  other arithmetic  8.38 us (11%)
  local copies, waits for them, and re-layouts  6.45 us (8%)
  between operations  1.56 us (2%)
    pallas_call x2, Pallas kernels, call(): pl.pallas_call(kernel, out_shape=[jax.ShapeDtypeStruct(*one) for one in s...  46.1 us
    dot_general x1, matrix products, body(): jnp.einsum('pk,bkc->bpc', weights, picked, preferred_element_type=jnp.flo...  3.74 us
    dot_general x1, matrix products, body(): jnp.einsum('pk,bpc->bkc', weights, grad_field, preferred_element_type=jnp...  3.3 us
    unnamed x7, local copies, waits for them, and re-layouts  3.07 us
    dot_general x1, matrix products, body(): mixed = jnp.dot(active_all, own_cols, preferred_element_type=jnp.float32)  2.05 us
    dot_general x1, matrix products, body(): jnp.einsum('tn,atkc->ankc', recv_pick, grad_terms, preferred_element_type...  1.58 us

profile of v2, /device:TPU:0, one launch (start us, length us, event | category | flops | bytes accessed | tf_op | source)
XLA Modules:
  0.0 76.5 jit_solution(15591070188099798815)
XLA Ops:
  0.6 1.0 %copy-done = bf16[1,256,8,128]{3,2,1,0:T(8,128)(2,1)S(1)} copy-done((bf16[1,256,8,128]{3,2,1,0:T(8,128)(2,1)S(1)}, bf16[1,256,8,128]{3,2,1,0:T(8,128)(2,1)}, u32[]{:S(2)}) %copy-start) | copy-done | bytes 524312
  1.7 0.7 broadcast_add_fusion
  2.4 0.8 %fusion.59 = pred[8,256]{1,0:T(8,128)(4,1)S(1)} fusion(s32[8,256]{1,0:T(8,128)} %param.11, s32[]{:T(128)S(6)} %axis_index.23, s32[8]{0:T(128)} %param.13), kind=kLoop, calls=%fused_computation.97 | loop fusion | flops 6144 | bytes 10276 | tf_op jit(solution)/shard_map/and | solution.py:260
  4.6 0.9 %copy-done.1 = bf16[1,1024,128]{2,1,0:T(8,128)(2,1)S(1)} copy-done((bf16[1,1024,128]{2,1,0:T(8,128)(2,1)S(1)}, bf16[1,1024,128]{2,1,0:T(8,128)(2,1)}, u32[]{:S(2)}) %copy-start.1) | copy-done | bytes 262168
  5.5 24.3 %shard_map.120 = (bf16[3072,128]{1,0:T(8,128)(2,1)S(1)}, bf16[1024,512]{1,0:T(8,128)(2,1)S(1)}) custom-call(bf16[3072,128]{1,0:T(8,128)(2,1)S(1)} %bitcast.121, bf16[1024,128]{1,0:T(8,128)(2,1)S(1)} %bitcast.125), custom_call_target="tpu_custom_call" | custom-call | tf_op jit(solution)/shard_map/pallas_call | solution.py:218
  29.8 0.8 %select_reduce_fusion.1 = s32[256]{0:T(256)S(1)} fusion(s32[8,256]{1,0:T(8,128)} %param.11, pred[8]{0:T(512)(128)(4,1)S(1)} %iota_compare_fusion.8), kind=kLoop, calls=%fused_computation.95 | loop fusion | flops 3840 | bytes 9224 | tf_op jit(solution)/shard_map/reduce_sum | solution.py:272
  30.6 1.3 %select_reduce_fusion.2 = s32[]{:T(128)} fusion(s32[8]{0:T(128)} %param.13, s32[]{:T(128)S(6)} %axis_index.23), kind=kLoop, calls=%fused_computation.122 | loop fusion | flops 23 | bytes 40 | tf_op jit(solution)/shard_map/reduce_sum | solution.py:273
  31.9 0.6 iota_compare_fusion.7
  32.8 0.7 add_select_fusion
  33.4 0.5 fusion.18
  34.3 3.7 %fusion.13 = bf16[1,1156,128]{2,1,0:T(8,128)(2,1)S(1)} fusion(bf16[1,1156,2048]{2,1,0:T(8,128)(2,1)} %param.10, bf16[1,256,8,128]{3,2,1,0:T(8,128)(2,1)S(1)} %copy.58), kind=kOutput, calls=%fused_computation.7 | convolution fusion | flops 606224896 | bytes 5555200 | tf_op jit(solution)/shard_map/pk,bkc->bpc/dot_general | solution.py:305
  38.9 1.3 %fusion.57 = f32[1024,128]{1,0:T(8,128)S(1)} fusion(bf16[1024,512]{1,0:T(8,128)(2,1)S(1)} %get-tuple-element.10, bf16[512,512]{1,0:T(8,128)(2,1)} %param.16, s32[]{:T(128)S(6)} %select_n.82), kind=kOutput, calls=%fused_computation.92 | convolution fusion | flops 134217728 | bytes 1703940 | tf_op jit(solution)/shard_map/dot_general | solution.py:314
  40.3 0.9 %fusion.32 = (f32[128]{0:T(128)S(1)}, f32[128]{0:T(128)S(1)}, f32[128]{0:T(128)S(1)}, f32[128]{0:T(128)S(1)}, f32[128]{0:T(128)S(1)}, /*index=5*/f32[128]{0:T(12...) fusion(bf16[1,34,34,128]{3,2,1,0:T(8,128)(2,1)S(1)} %reshape.15, ...), kind=kLoop, calls=%fused_computation.50 | loop fusion | flops 6814592 | bytes 3941376 | tf_op jit(solution)/shard_map/reduce_sum | solution.py:43
  41.2 0.7 broadcast_multiply_fusion.8
  41.9 0.7 add_convert_fusion
  42.7 3.3 %fusion.10 = bf16[1,2048,128]{1,2,0:T(8,128)(2,1)S(1)} fusion(bf16[1156,128]{1,0:T(8,128)(2,1)S(1)} %reshape.151, bf16[1,1156,2048]{2,1,0:T(8,128)(2,1)} %param.10), kind=kOutput, calls=%fused_computation.6 | convolution fusion | flops 606339072 | bytes 5555200 | tf_op jit(solution)/shard_map/pk,bpc->bkc/dot_general | solution.py:326
  46.0 1.0 %copy.59 = bf16[1,2048,128]{2,1,0:T(8,128)(2,1)} copy(bf16[1,2048,128]{1,2,0:T(8,128)(2,1)S(1)} %fusion.10) | data formatting | bytes 1048576 | tf_op jit(solution)/shard_map/convert_element_type | solution.py:327
  47.0 1.6 %fusion.17 = bf16[1,384,8,128]{1,3,2,0:T(8,128)(2,1)S(1)} fusion(bf16[256,8,128]{2,1,0:T(8,128)(2,1)} %bitcast.127, s32[256]{0:T(256)S(1)} %add_select_fusion), kind=kOutput, calls=%fused_computation.13 | convolution fusion | flops 201818112 | bytes 1311744 | tf_op jit(solution)/shard_map/tn,atkc->ankc/dot_general | solution.py:328
  49.6 21.8 %shard_map.121 = (bf16[3072,128]{1,0:T(8,128)(2,1)S(1)}, bf16[1024,512]{1,0:T(8,128)(2,1)S(1)}, bf16[512,128]{1,0:T(8,128)(2,1)S(1)}, f32[16,128]{1,0:T(8,128)S(1)}) custom-call(bf16[3072,128]{1,0:T(8,128)(2,1)S(1)} %bitcast.120, bf16[1024,128]{1,0:T(8,128)(2,1)S(1)} %bitcast.123, f32[512,128]{1,0:T(8,128)S(1)} %pad_maximum_fusion.mix_ref, ...), custom_call_target="tpu_custom_call" | custom-call | tf_op jit(solution)/shard_map/pallas_call | solution.py:218
  71.4 2.1 %fusion.20 = bf16[1,1024,128]{2,1,0:T(8,128)(2,1)} fusion(bf16[1024,512]{1,0:T(8,128)(2,1)S(1)} %get-tuple-element.12, bf16[512,512]{1,0:T(8,128)(2,1)} %param.16, s32[]{:T(128)S(6)} %select_n.82), kind=kOutput, calls=%fused_computation.17 | convolution fusion | flops 134348800 | bytes 1441796 | tf_op jit(solution)/shard_map/dot_general | solution.py:358
  73.5 0.5 fusion.19
  74.0 1.1 %copy.70 = bf16[1,256,8,128]{3,2,1,0:T(8,128)(2,1)} copy(bf16[1,256,8,128]{1,3,2,0:T(8,128)(2,1)S(1)} %fusion.19) | data formatting | bytes 1048576
  75.1 0.6 mul.267
  75.7 0.7 maximum_multiply_fusion
  (37 shorter events, 3.2 us)
Async XLA Ops:
  0.6 1.0 %copy-start = (bf16[1,256,8,128]{3,2,1,0:T(8,128)(2,1)S(1)}, bf16[1,256,8,128]{3,2,1,0:T(8,128)(2,1)}, u32[]{:S(2)}) copy-start(bf16[1,256,8,128]{3,2,1,0:T(8,128)(2,1)} %param.9) | copy-start | bytes 1572868
  4.6 1.0 %copy-start.1 = (bf16[1,1024,128]{2,1,0:T(8,128)(2,1)S(1)}, bf16[1,1024,128]{2,1,0:T(8,128)(2,1)}, u32[]{:S(2)}) copy-start(bf16[1,1024,128]{2,1,0:T(8,128)(2,1)} %param.17) | copy-start | bytes 786436
  5.5 32.6 %copy-start.2 = (bf16[3,3,128]{2,1,0:T(4,128)(2,1)S(1)}, bf16[3,3,128]{2,1,0:T(4,128)(2,1)}, u32[]{:S(2)}) copy-start(bf16[3,3,128]{2,1,0:T(4,128)(2,1)} %param.15) | copy-start | bytes 6916

commit v3 on v2

--- a/solution.py
+++ b/solution.py
@@ -99,7 +99,7 @@
         copy.wait()
 
 
-def line_gather(own, full, sems, local_sem, after=None):
+def line_gather(own, full, sems, local_sem, between):
     total, here = lax.axis_size("chan"), lax.axis_index("chan")
     wide, rows = own.shape[1], own.shape[0] // CHUNKS
 
@@ -145,8 +145,8 @@
                     def _(way=way, step=step, chunk=chunk):
                         hop(way, step, chunk).start()
 
-        if step == 1 and after is not None:
-            after()
+        if step in between:
+            between[step]()
     for step in range(total - 1):
         for chunk in range(CHUNKS):
             for way in range(2):
@@ -158,17 +158,54 @@
     local.wait()
 
 
-def first_kernel(out_ref, own_ref, in_ref, full_ref, swap_sems, line_sems, local_sem):
+def first_kernel(
+    out_ref,
+    own_ref,
+    pick_ref,
+    weights_ref,
+    in_ref,
+    full_ref,
+    mapped_ref,
+    weights,
+    slots,
+    picked,
+    swap_sems,
+    line_sems,
+    local_sem,
+    weights_sem,
+):
+    fetch = pltpu.make_async_copy(weights_ref, weights, weights_sem)
+    fetch.start()
     greet()
     rows = out_ref.shape[0] // lax.axis_size("tile")
     copies = swap_start(out_ref, in_ref, rows, swap_sems, False)
-    line_gather(own_ref, full_ref, line_sems, local_sem)
-    wait_all(copies)
+    terms, filled = pick_ref.shape
+    seg = out_ref.shape[0] // filled
+
+    def remap():
+        wait_all(copies)
+        slots[...] = in_ref[...].astype(jnp.float32)
+        for point in range(seg):
+            part = slots[pl.ds(point, filled, stride=seg), :].astype(jnp.bfloat16)
+            picked[pl.ds(point, terms, stride=seg), :] = jnp.dot(
+                pick_ref[...], part, preferred_element_type=jnp.float32
+            )
+        fetch.wait()
+        mapped_ref[...] = jnp.dot(
+            weights[...],
+            picked[...].astype(jnp.bfloat16),
+            preferred_element_type=jnp.float32,
+        ).astype(jnp.bfloat16)
+
+    last = lax.axis_size("chan") - 2
+    line_gather(own_ref, full_ref, line_sems, local_sem, {last: remap})
 
 
 def second_kernel(
-    out_ref,
+    grad_ref,
     own_ref,
+    pick_ref,
+    weights_ref,
     mix_ref,
     taps_ref,
     in_ref,
@@ -178,20 +215,49 @@
     mix_parts,
     mix_own,
     taps_parts,
+    weights,
+    terms_ref,
+    slots,
+    out_ref,
     swap_sems,
     line_sems,
     mix_sems,
     back_sems,
     taps_sems,
     local_sem,
+    weights_sem,
 ):
+    fetch = pltpu.make_async_copy(weights_ref, weights, weights_sem)
+    fetch.start()
     greet()
     total = lax.axis_size("tile")
     mix_rows = mix_ref.shape[0] // total
     mix_copies = swap_start(mix_ref, mix_parts, mix_rows, mix_sems, False)
     taps_copies = swap_start(taps_ref, taps_parts, taps_ref.shape[0], taps_sems, True)
-    copies = swap_start(out_ref, in_ref, out_ref.shape[0] // total, swap_sems, False)
-    back = []
+    copies, back = [], []
+    terms, filled = pick_ref.shape
+    seg = out_ref.shape[0] // filled
+
+    def unmap():
+        fetch.wait()
+        turned = lax.dot_general(
+            grad_ref[...],
+            weights[...],
+            (((0,), (0,)), ((), ())),
+            preferred_element_type=jnp.float32,
+        )
+        terms_ref[...] = turned.T
+        for point in range(seg):
+            part = terms_ref[pl.ds(point, terms, stride=seg), :].astype(jnp.bfloat16)
+            slots[pl.ds(point, filled, stride=seg), :] = lax.dot_general(
+                pick_ref[...],
+                part,
+                (((0,), (0,)), ((), ())),
+                preferred_element_type=jnp.float32,
+            )
+        out_ref[...] = slots[...].astype(jnp.bfloat16)
+        rows = out_ref.shape[0] // total
+        copies.extend(swap_start(out_ref, in_ref, rows, swap_sems, False))
 
     def reduce():
         wait_all(mix_copies)
@@ -201,7 +267,7 @@
         mix_own[...] = summed.astype(mix_own.dtype)
         back.extend(swap_start(mix_own, mix_out, mix_rows, back_sems, True))
 
-    line_gather(own_ref, full_ref, line_sems, local_sem, reduce)
+    line_gather(own_ref, full_ref, line_sems, local_sem, {0: unmap, 1: reduce})
     wait_all(taps_copies)
     tap_rows = taps_ref.shape[0]
     taps = taps_parts[0:tap_rows]
@@ -218,7 +284,10 @@
     return pl.pallas_call(
         kernel,
         out_shape=[jax.ShapeDtypeStruct(*one) for one in shapes],
-        in_specs=[vmem] * len(operands),
+        in_specs=[
+            pl.BlockSpec(memory_space=pl.ANY) if at == 3 else vmem
+            for at in range(len(operands))
+        ],
         out_specs=[vmem] * len(shapes),
         scratch_shapes=[
             *[pltpu.VMEM(*one) for one in scratch],
@@ -226,11 +295,12 @@
             pltpu.SemaphoreType.DMA(line),
             *[pltpu.SemaphoreType.DMA((2, lax.axis_size("tile")))] * sems,
             pltpu.SemaphoreType.DMA,
+            pltpu.SemaphoreType.DMA,
         ],
         compiler_params=pltpu.CompilerParams(
             collective_id=collective_id,
             has_side_effects=True,
-            vmem_limit_bytes=24 * 2**20,
+            vmem_limit_bytes=40 * 2**20,
         ),
     )(*operands)
 
@@ -289,21 +359,26 @@
     chan_total = lax.axis_size("chan")
     outgoing = outgoing.reshape(-1, chan_local)
     whole_shape = (flat_rows, chan_total * chan_local)
-    arrived, piece = call(
+    points = (term_pts, chan_local)
+    _, piece, remapped = call(
         first_kernel,
-        ((outgoing.shape, jnp.bfloat16), (whole_shape, jnp.bfloat16)),
-        (),
+        (
+            (outgoing.shape, jnp.bfloat16),
+            (whole_shape, jnp.bfloat16),
+            ((ext_cells, chan_local), jnp.bfloat16),
+        ),
+        (
+            (weights.shape, jnp.bfloat16),
+            (outgoing.shape, jnp.float32),
+            (points, jnp.float32),
+        ),
         0,
         0,
         outgoing,
         upstream,
-    )
-    arrived = arrived.reshape(slot_shape)
-    picked = jnp.einsum("tn,ankc->atkc", recv_pick, arrived, preferred_element_type=jnp.float32)
-    picked = picked.astype(jnp.bfloat16)
-    picked = picked.reshape(picked.shape[0], term_pts, chan_local)
-    mapped = jnp.einsum("pk,bkc->bpc", weights, picked, preferred_element_type=jnp.float32)
-    remapped = mapped.astype(jnp.bfloat16)
+        recv_pick,
+        weights,
+    )
     field = remapped.reshape(batch_rows, ext_edge, ext_edge, chan_local)
     turn = rotation[0]
     kernel = turn_kernel(depthwise.astype(jnp.float32), turn, 1)
@@ -322,23 +397,18 @@
     sigma = jax.nn.sigmoid(hidden)
     grad_hidden = grad_active.reshape(hidden.shape) * sigma * (1.0 + hidden * (1.0 - sigma))
     grad_turned, grad_field = stencil_grads(field, kernel, grad_hidden)
-    grad_field = grad_field.astype(jnp.bfloat16).reshape(batch_rows, ext_cells, chan_local)
-    grad_terms = jnp.einsum("pk,bpc->bkc", weights, grad_field, preferred_element_type=jnp.float32)
-    grad_terms = grad_terms.astype(jnp.bfloat16).reshape(batch_rows, terms_max, seg_len, chan_local)
-    returning = jnp.einsum("tn,atkc->ankc", recv_pick, grad_terms, preferred_element_type=jnp.float32)
-    returning = returning.astype(jnp.bfloat16)
+    grad_field = grad_field.astype(jnp.bfloat16).reshape(ext_cells, chan_local)
     grad_kernel = turn_kernel(grad_turned, turn, -1).reshape(9, chan_local)
     grad_kernel = jnp.pad(grad_kernel, ((0, 7), (0, 0)))
     grad_mix = jnp.concatenate(
         [grad_mix[:, i * chan_local : (i + 1) * chan_local] for i in range(chan_total)]
     )
-    returning = returning.reshape(-1, chan_local)
     mix_rows = grad_mix.shape[0] // tile_total
     mix_type = jnp.bfloat16 if mix_rows % 16 == 0 else jnp.float32
     arrived, active_all, mix_sum, kernel_sum = call(
         second_kernel,
         (
-            (returning.shape, jnp.bfloat16),
+            (outgoing.shape, jnp.bfloat16),
             (whole_shape, jnp.bfloat16),
             (grad_mix.shape, mix_type),
             (grad_kernel.shape, jnp.float32),
@@ -347,11 +417,17 @@
             (grad_mix.shape, jnp.float32),
             ((mix_rows, chan_local), mix_type),
             ((tile_total * grad_kernel.shape[0], chan_local), jnp.float32),
+            (weights.shape, jnp.bfloat16),
+            (points, jnp.float32),
+            (outgoing.shape, jnp.float32),
+            (outgoing.shape, jnp.bfloat16),
         ),
         3,
         1,
-        returning,
+        grad_field,
         active,
+        recv_pick,
+        weights,
         grad_mix,
         grad_kernel,
     )

time: 77 us -> 70.3 us (0.913)
  matrix products: 14 us -> 3.04 us
  local copies, waits for them, and re-layouts: 6.45 us -> 9.31 us
  Pallas kernels: 46.1 us -> 47.5 us
    dot_general x4 -> x0, matrix products: 9.16 us -> none  [the longest x1 3.74 us: body(): jnp.einsum('pk,bkc->bpc', weights, picked, preferred_element_type=jnp.flo...]
    unnamed x7 -> x13, local copies, waits for them, and re-layouts: 3.07 us -> 7.76 us
    convert_element_type x3 -> x0, local copies, waits for them, and re-layouts: 1.83 us -> none  [the longest x1 1 us: body(): grad_terms.astype(jnp.bfloat16)]
    pallas_call x2, Pallas kernels: 46.1 us -> 47.5 us  [call(): pl.pallas_call(kernel, out_shape=[jax.ShapeDtypeStruct(*one) for one in s...]
    dot_general x1, matrix products: 1.34 us -> 0.44 us  [body(): lax.dot_general(piece, own_rows, (((1,), (1,)), ((), ())), preferred_elem...]
    dot_general x1, matrix products: 2.05 us -> 1.15 us  [body(): mixed = jnp.dot(active_all, own_cols, preferred_element_type=jnp.float32)]
where the time goes in v3:
time: 70.3 us; the launch traced here: 69.9 us
  Pallas kernels  47.5 us (68%)
  local copies, waits for them, and re-layouts  9.31 us (13%)
  other arithmetic  8.49 us (12%)
  matrix products  3.04 us (4%)
  between operations  1.56 us (2%)
    pallas_call x2, Pallas kernels, call(): pl.pallas_call(kernel, out_shape=[jax.ShapeDtypeStruct(*one) for one in s...  47.5 us
    unnamed x13, local copies, waits for them, and re-layouts  7.76 us

profile of v3, /device:TPU:0, one launch (start us, length us, event | category | flops | bytes accessed | tf_op | source)
XLA Modules:
  0.0 69.9 jit_solution(7883425319012289471)
XLA Ops:
  0.6 1.0 %copy-done = bf16[1,256,8,128]{3,2,1,0:T(8,128)(2,1)S(1)} copy-done((bf16[1,256,8,128]{3,2,1,0:T(8,128)(2,1)S(1)}, bf16[1,256,8,128]{3,2,1,0:T(8,128)(2,1)}, u32[]{:S(2)}) %copy-start) | copy-done | bytes 524312
  1.7 0.7 broadcast_add_fusion
  2.4 0.8 %fusion.34 = pred[8,256]{1,0:T(8,128)(4,1)S(1)} fusion(s32[8,256]{1,0:T(8,128)} %param.11, s32[]{:T(128)S(6)} %axis_index.23, s32[8]{0:T(128)} %param.13), kind=kLoop, calls=%fused_computation.80 | loop fusion | flops 6144 | bytes 10276 | tf_op jit(solution)/shard_map/and | solution.py:330
  3.6 0.4 fusion
  4.1 0.5 copy.72
  4.6 0.8 %select_reduce_fusion.1 = s32[256]{0:T(256)S(1)} fusion(s32[8,256]{1,0:T(8,128)} %param.11, pred[8]{0:T(512)(128)(4,1)S(1)} %iota_compare_fusion.8), kind=kLoop, calls=%fused_computation.78 | loop fusion | flops 3840 | bytes 9224 | tf_op jit(solution)/shard_map/reduce_sum | solution.py:342
  5.4 1.3 %select_reduce_fusion.2 = s32[]{:T(128)} fusion(s32[8]{0:T(128)} %param.13, s32[]{:T(128)S(6)} %axis_index.23), kind=kLoop, calls=%fused_computation.105 | loop fusion | flops 23 | bytes 40 | tf_op jit(solution)/shard_map/reduce_sum | solution.py:343
  6.7 0.6 iota_compare_fusion.7
  7.5 0.7 add_select_fusion
  8.3 2.3 %copy-done.1 = bf16[1,1156,2048]{2,1,0:T(8,128)(2,1)S(1)} copy-done((bf16[1,1156,2048]{2,1,0:T(8,128)(2,1)S(1)}, bf16[1,1156,2048]{2,1,0:T(8,128)(2,1)}, u32[]{:S(2)}) %copy-start.1) | copy-done | bytes 4735000
  10.6 0.9 %copy-done.3 = bf16[1,1024,128]{2,1,0:T(8,128)(2,1)S(1)} copy-done((bf16[1,1024,128]{2,1,0:T(8,128)(2,1)S(1)}, bf16[1,1024,128]{2,1,0:T(8,128)(2,1)}, u32[]{:S(2)}) %copy-start.3) | copy-done | bytes 262168
  11.6 25.5 %shard_map.120 = (bf16[3072,128]{1,0:T(8,128)(2,1)}, bf16[1024,512]{1,0:T(8,128)(2,1)S(1)}, bf16[1156,128]{1,0:T(8,128)(2,1)S(1)}) custom-call(bf16[3072,128]{1,0:T(8,128)(2,1)S(1)} %bitcast.83, bf16[1024,128]{1,0:T(8,128)(2,1)S(1)} %bitcast.87, bf16[256,384]{1,0:T(8,128)(2,1)S(1)} %fusion.27.pick_ref, bf16[1156,2048]{1,0:T(8,128)(2,1)S(1)} %bitcast.81), custom_call_target="tpu_custom_call" | custom-call | tf_op jit(solution)/shard_map/pallas_call | solution.py:284
  38.0 0.4 fusion.32
  38.4 0.9 %fusion.13 = (f32[128]{0:T(128)S(1)}, f32[128]{0:T(128)S(1)}, f32[128]{0:T(128)S(1)}, f32[128]{0:T(128)S(1)}, f32[128]{0:T(128)S(1)}, /*index=5*/f32[128]{0:T(12...) fusion(bf16[1,34,34,128]{3,2,1,0:T(8,128)(2,1)S(1)} %reshape.12, ...), kind=kLoop, calls=%fused_computation.37 | loop fusion | flops 6814592 | bytes 3941376 | tf_op jit(solution)/shard_map/reduce_sum | solution.py:43
  39.4 0.7 broadcast_multiply_fusion.8
  40.1 0.7 add_convert_fusion
  40.9 0.3 fusion.43
  41.4 2.3 %copy-done.2 = bf16[1,1156,2048]{2,1,0:T(8,128)(2,1)S(1)} copy-done((bf16[1,1156,2048]{2,1,0:T(8,128)(2,1)S(1)}, bf16[1,1156,2048]{2,1,0:T(8,128)(2,1)}, u32[]{:S(2)}) %copy-start.2) | copy-done | bytes 4735000
  43.8 22.0 %shard_map.121 = (bf16[3072,128]{1,0:T(8,128)(2,1)S(1)}, bf16[1024,512]{1,0:T(8,128)(2,1)S(1)}, bf16[512,128]{1,0:T(8,128)(2,1)S(1)}, f32[16,128]{1,0:T(8,128)S(1)}) custom-call(bf16[1156,128]{1,0:T(8,128)(2,1)S(1)} %reshape.121.grad_ref, bf16[1024,128]{1,0:T(8,128)(2,1)S(1)} %bitcast.85, bf16[256,384]{1,0:T(8,128)(2,1)S(1)} %fusion.27.pick_ref, ...), custom_call_target="tpu_custom_call" | custom-call | tf_op jit(solution)/shard_map/pallas_call | solution.py:284
  65.7 1.2 %fusion.2 = bf16[1,1024,128]{2,1,0:T(8,128)(2,1)} fusion(bf16[1024,512]{1,0:T(8,128)(2,1)S(1)} %get-tuple-element.12, bf16[512,512]{1,0:T(8,128)(2,1)S(1)} %copy-done.4, s32[]{:T(128)S(6)} %select_n.85), kind=kOutput, calls=%fused_computation.5 | convolution fusion | flops 134348800 | bytes 1441796 | tf_op jit(solution)/shard_map/dot_general | solution.py:434
  66.9 0.6 fusion.1
  67.5 1.1 %copy.42 = bf16[1,256,8,128]{3,2,1,0:T(8,128)(2,1)} copy(bf16[1,256,8,128]{1,3,2,0:T(8,128)(2,1)S(1)} %fusion.1) | data formatting | bytes 1048576
  68.5 0.6 mul.267
  69.2 0.7 %maximum_multiply_fusion = f32[128,512]{1,0:T(8,128)} fusion(f32[128,128]{1,0:T(8,128)S(1)} %get-tuple-element.51, f32[128,128]{1,0:T(8,128)S(1)} %get-tuple-element.50, f32[128,128]{1,0:T(8,128)S(1)} %get-tuple-element.49, f32[128,128]{1,0:T(8,128)S(1)} %get-tuple-element.48), kind=kLoop, calls=%fused_computation.58 | loop fusion | flops 262144 | bytes 524288 | tf_op jit(solution)/shard_map/mul | solution.py:445
  (37 shorter events, 1.2 us)
Async XLA Ops:
  0.6 1.0 %copy-start = (bf16[1,256,8,128]{3,2,1,0:T(8,128)(2,1)S(1)}, bf16[1,256,8,128]{3,2,1,0:T(8,128)(2,1)}, u32[]{:S(2)}) copy-start(bf16[1,256,8,128]{3,2,1,0:T(8,128)(2,1)} %param.9) | copy-start | bytes 1572868
  3.6 33.6 %copy-start.5 = (bf16[3,3,128]{2,1,0:T(4,128)(2,1)S(1)}, bf16[3,3,128]{2,1,0:T(4,128)(2,1)}, u32[]{:S(2)}) copy-start(bf16[3,3,128]{2,1,0:T(4,128)(2,1)} %param.15) | copy-start | bytes 6916
  3.6 34.4 %copy-start.4 = (bf16[512,512]{1,0:T(8,128)(2,1)S(1)}, bf16[512,512]{1,0:T(8,128)(2,1)}, u32[]{:S(2)}) copy-start(bf16[512,512]{1,0:T(8,128)(2,1)} %param.16) | copy-start | bytes 1572868
  8.3 2.3 %copy-start.1 = (bf16[1,1156,2048]{2,1,0:T(8,128)(2,1)S(1)}, bf16[1,1156,2048]{2,1,0:T(8,128)(2,1)}, u32[]{:S(2)}) copy-start(bf16[1,1156,2048]{2,1,0:T(8,128)(2,1)} %param.10) | copy-start | bytes 14204932
  10.6 0.9 %copy-start.3 = (bf16[1,1024,128]{2,1,0:T(8,128)(2,1)S(1)}, bf16[1,1024,128]{2,1,0:T(8,128)(2,1)}, u32[]{:S(2)}) copy-start(bf16[1,1024,128]{2,1,0:T(8,128)(2,1)} %param.17) | copy-start | bytes 786436
  41.4 2.3 %copy-start.2 = (bf16[1,1156,2048]{2,1,0:T(8,128)(2,1)S(1)}, bf16[1,1156,2048]{2,1,0:T(8,128)(2,1)}, u32[]{:S(2)}) copy-start(bf16[1,1156,2048]{2,1,0:T(8,128)(2,1)} %param.10) | copy-start | bytes 14204932

commit v4 on v3

--- a/solution.py
+++ b/solution.py
@@ -161,11 +161,13 @@
 def first_kernel(
     out_ref,
     own_ref,
-    pick_ref,
+    source_ref,
     weights_ref,
+    column_ref,
     in_ref,
     full_ref,
     mapped_ref,
+    pick_ref,
     weights,
     slots,
     picked,
@@ -183,6 +185,18 @@
     seg = out_ref.shape[0] // filled
 
     def remap():
+        shape = (terms, terms)
+        source = column_ref[...]
+        earlier = lax.broadcasted_iota(jnp.int32, shape, 1) <= lax.broadcasted_iota(
+            jnp.int32, shape, 0
+        )
+        same = (source == source_ref[...]) & earlier
+        rank = jnp.sum(jnp.where(same, 1.0, 0.0), axis=1, keepdims=True) - 1.0
+        capacity = filled // lax.axis_size("tile")
+        slot = source.astype(jnp.float32) * capacity + rank
+        slot = jnp.where(source >= 0, slot, -1.0)
+        ids = lax.broadcasted_iota(jnp.int32, (terms, filled), 1).astype(jnp.float32)
+        pick_ref[...] = jnp.where(slot == ids, 1.0, 0.0).astype(jnp.bfloat16)
         wait_all(copies)
         slots[...] = in_ref[...].astype(jnp.float32)
         for point in range(seg):
@@ -285,7 +299,7 @@
         kernel,
         out_shape=[jax.ShapeDtypeStruct(*one) for one in shapes],
         in_specs=[
-            pl.BlockSpec(memory_space=pl.ANY) if at == 3 else vmem
+            pl.BlockSpec(memory_space=pltpu.HBM) if at == 3 else vmem
             for at in range(len(operands))
         ],
         out_specs=[vmem] * len(shapes),
@@ -300,7 +314,7 @@
         compiler_params=pltpu.CompilerParams(
             collective_id=collective_id,
             has_side_effects=True,
-            vmem_limit_bytes=40 * 2**20,
+            vmem_limit_bytes=52 * 2**20,
         ),
     )(*operands)
 
@@ -342,15 +356,7 @@
     own_source = jnp.sum(jnp.where(tile_mask, term_source, 0), axis=0)
     own_count = jnp.sum(jnp.where(tile_mask[:, 0], term_count, 0))
     own_use = positions < own_count
-    same_source = (
-        (own_source[None, :] == own_source[:, None])
-        & own_use[None, :]
-        & (positions[None, :] <= positions[:, None])
-    )
-    own_rank = jnp.sum(same_source.astype(jnp.int32), axis=1) - 1
-    recv_slot = jnp.where(own_use, own_source * capacity + own_rank, -1)
-    slots = jnp.arange(tile_total * capacity, dtype=jnp.int32)
-    recv_pick = (recv_slot[:, None] == slots[None, :]).astype(jnp.bfloat16)
+    named = jnp.where(own_use, own_source, -1)
     weights = remap_weights[0]
     ext_cells = weights.shape[0]
     term_pts = weights.shape[1]
@@ -360,12 +366,13 @@
     outgoing = outgoing.reshape(-1, chan_local)
     whole_shape = (flat_rows, chan_total * chan_local)
     points = (term_pts, chan_local)
-    _, piece, remapped = call(
+    _, piece, remapped, recv_pick = call(
         first_kernel,
         (
             (outgoing.shape, jnp.bfloat16),
             (whole_shape, jnp.bfloat16),
             ((ext_cells, chan_local), jnp.bfloat16),
+            ((terms_max, tile_total * capacity), jnp.bfloat16),
         ),
         (
             (weights.shape, jnp.bfloat16),
@@ -376,8 +383,9 @@
         0,
         outgoing,
         upstream,
-        recv_pick,
+        named[None, :],
         weights,
+        named[:, None],
     )
     field = remapped.reshape(batch_rows, ext_edge, ext_edge, chan_local)
     turn = rotation[0]

time: 70.3 us -> 70.6 us (level)
  local copies, waits for them, and re-layouts: 9.31 us -> 5.67 us
  matrix products: 3.04 us -> 5.5 us
  Pallas kernels: 47.5 us -> 49.3 us
    unnamed x13 -> x9, local copies, waits for them, and re-layouts: 7.76 us -> 3.07 us
    pallas_call x2, Pallas kernels: 47.5 us -> 49.3 us  [call(): pl.pallas_call(kernel, out_shape=[jax.ShapeDtypeStruct(*one) for one in s...]
    dot_general x1, matrix products: 0.44 us -> 1.66 us  [body(): lax.dot_general(piece, own_rows, (((1,), (1,)), ((), ())), preferred_elem...]
    dot_general x1, matrix products: 1.15 us -> 2.37 us  [body(): mixed = jnp.dot(active_all, own_cols, preferred_element_type=jnp.float32)]
    convert_element_type x1, local copies, waits for them, and re-layouts: 0.51 us -> 1.44 us  [body(): outgoing = outgoing.astype(jnp.bfloat16)]
where the time goes in v4:
time: 70.6 us; the launch traced here: 70.2 us
  Pallas kernels  49.3 us (70%)
  other arithmetic  8.21 us (12%)
  local copies, waits for them, and re-layouts  5.67 us (8%)
  matrix products  5.5 us (8%)
  between operations  1.53 us (2%)
    pallas_call x2, Pallas kernels, call(): pl.pallas_call(kernel, out_shape=[jax.ShapeDtypeStruct(*one) for one in s...  49.3 us
    unnamed x9, local copies, waits for them, and re-layouts  3.07 us
    dot_general x1, matrix products, body(): mixed = jnp.dot(active_all, own_cols, preferred_element_type=jnp.float32)  2.37 us
    dot_general x1, matrix products, body(): lax.dot_general(piece, own_rows, (((1,), (1,)), ((), ())), preferred_elem...  1.66 us
    convert_element_type x1, local copies, waits for them, and re-layouts, body(): outgoing = outgoing.astype(jnp.bfloat16)  1.44 us

profile of v4, /device:TPU:0, one launch (start us, length us, event | category | flops | bytes accessed | tf_op | source)
XLA Modules:
  0.0 70.2 jit_solution(9423315808548965449)
XLA Ops:
  0.6 1.0 %copy-done = bf16[1,256,8,128]{3,2,1,0:T(8,128)(2,1)S(1)} copy-done((bf16[1,256,8,128]{3,2,1,0:T(8,128)(2,1)S(1)}, bf16[1,256,8,128]{3,2,1,0:T(8,128)(2,1)}, u32[]{:S(2)}) %copy-start) | copy-done | bytes 524312
  1.7 0.7 broadcast_add_fusion
  2.4 0.8 %fusion.33 = pred[8,256]{1,0:T(8,128)(4,1)S(1)} fusion(s32[8,256]{1,0:T(8,128)} %param.11, s32[]{:T(128)S(6)} %axis_index.23, s32[8]{0:T(128)} %param.13), kind=kLoop, calls=%fused_computation.77 | loop fusion | flops 6144 | bytes 10276 | tf_op jit(solution)/shard_map/and | solution.py:344
  3.1 0.1 fusion.3
  3.3 0.2 select_reduce_fusion
  3.6 0.4 fusion
  4.1 1.4 %copy.89 = bf16[1,384,8,128]{3,2,1,0:T(8,128)(2,1)} copy(bf16[1,384,8,128]{3,1,2,0:T(8,128)(2,1)S(1)} %fusion) | data formatting | bytes 1572864 | tf_op jit(solution)/shard_map/convert_element_type | solution.py:354
  5.5 0.8 %select_reduce_fusion.1 = s32[256]{0:T(256)S(1)} fusion(s32[8,256]{1,0:T(8,128)} %param.11, pred[8]{0:T(512)(128)(4,1)S(1)} %iota_compare_fusion.6), kind=kLoop, calls=%fused_computation.75 | loop fusion | flops 3840 | bytes 9224 | tf_op jit(solution)/shard_map/reduce_sum | solution.py:356
  6.3 1.3 %select_reduce_fusion.2 = s32[]{:T(128)} fusion(s32[8]{0:T(128)} %param.13, s32[]{:T(128)S(6)} %axis_index.23), kind=kLoop, calls=%fused_computation.101 | loop fusion | flops 23 | bytes 40 | tf_op jit(solution)/shard_map/reduce_sum | solution.py:357
  7.6 0.6 compare_select_fusion.source_ref
  8.4 0.7 fusion.32.column_ref
  9.1 0.9 %copy-done.1 = bf16[1,1024,128]{2,1,0:T(8,128)(2,1)S(1)} copy-done((bf16[1,1024,128]{2,1,0:T(8,128)(2,1)S(1)}, bf16[1,1024,128]{2,1,0:T(8,128)(2,1)}, u32[]{:S(2)}) %copy-start.1) | copy-done | bytes 262168
  10.0 26.6 %shard_map.120 = (bf16[3072,128]{1,0:T(8,128)(2,1)}, bf16[1024,512]{1,0:T(8,128)(2,1)}, bf16[1156,128]{1,0:T(8,128)(2,1)S(1)}, bf16[256,384]{1,0:T(8,128)(2,1)S(1)}) custom-call(bf16[3072,128]{1,0:T(8,128)(2,1)} %bitcast.89, bf16[1024,128]{1,0:T(8,128)(2,1)S(1)} %bitcast.86, s32[1,256]{1,0:T(1,128)S(1)} %compare_select_fusion.source_ref, ...), custom_call_target="tpu_custom_call" | custom-call | tf_op jit(solution)/shard_map/pallas_call | solution.py:298
  37.5 1.7 %fusion.30 = f32[1024,128]{1,0:T(8,128)S(1)} fusion(bf16[1024,512]{1,0:T(8,128)(2,1)} %get-tuple-element.11, bf16[512,512]{1,0:T(8,128)(2,1)} %param.16, s32[]{:T(128)S(6)} %select_n.98), kind=kOutput, calls=%fused_computation.70 | convolution fusion | flops 134217728 | bytes 1703940 | tf_op jit(solution)/shard_map/dot_general | solution.py:397
  39.2 0.9 %fusion.13 = (f32[128]{0:T(128)S(1)}, f32[128]{0:T(128)S(1)}, f32[128]{0:T(128)S(1)}, f32[128]{0:T(128)S(1)}, f32[128]{0:T(128)S(1)}, /*index=5*/f32[128]{0:T(12...) fusion(bf16[1,34,34,128]{3,2,1,0:T(8,128)(2,1)S(1)} %reshape.13, ...), kind=kLoop, calls=%fused_computation.37 | loop fusion | flops 6814592 | bytes 3941376 | tf_op jit(solution)/shard_map/reduce_sum | solution.py:43
  40.1 0.6 broadcast_multiply_fusion.8
  40.8 0.7 %add_convert_fusion = bf16[1,34,34,128]{3,2,1,0:T(8,128)(2,1)S(1)} fusion(f32[1,32,32,128]{3,2,1,0:T(8,128)S(1)} %get-tuple-element.42, f32[1,32,32,128]{3,2,1,0:T(8,128)S(1)} %get-tuple-element.43, f32[1,32,32,128]{3,2,1,0:T(8,128)S(1)} %get-tuple-element.44, f32[1,32,32,128]{3,2,1,0:T(8,128)S(1)} %get-tuple-element.45, ...), kind=kLoop, calls=%fused_computation.10 | loop fusion | flops 1331712 | bytes 5014528 | tf_op jit(solution)/shard_map/convert_element_type | solution.py:408
  41.6 0.3 fusion.42
  42.2 22.6 %shard_map.121 = (bf16[3072,128]{1,0:T(8,128)(2,1)S(1)}, bf16[1024,512]{1,0:T(8,128)(2,1)}, bf16[512,128]{1,0:T(8,128)(2,1)S(1)}, f32[16,128]{1,0:T(8,128)S(1)}) custom-call(bf16[1156,128]{1,0:T(8,128)(2,1)S(1)} %reshape.131.grad_ref, bf16[1024,128]{1,0:T(8,128)(2,1)S(1)} %bitcast.84, bf16[256,384]{1,0:T(8,128)(2,1)S(1)} %get-tuple-element.13.pick_ref, ...), custom_call_target="tpu_custom_call" | custom-call | tf_op jit(solution)/shard_map/pallas_call | solution.py:298
  64.8 2.4 %fusion.2 = bf16[1,1024,128]{2,1,0:T(8,128)(2,1)} fusion(bf16[1024,512]{1,0:T(8,128)(2,1)} %get-tuple-element.14, bf16[512,512]{1,0:T(8,128)(2,1)} %param.16, s32[]{:T(128)S(6)} %select_n.98), kind=kOutput, calls=%fused_computation.5 | convolution fusion | flops 134348800 | bytes 1441796 | tf_op jit(solution)/shard_map/dot_general | solution.py:442
  67.2 0.5 fusion.1
  67.7 1.1 %copy.59 = bf16[1,256,8,128]{3,2,1,0:T(8,128)(2,1)} copy(bf16[1,256,8,128]{1,3,2,0:T(8,128)(2,1)S(1)} %fusion.1) | data formatting | bytes 1048576
  68.8 0.6 mul.255
  69.4 0.7 %maximum_multiply_fusion = f32[128,512]{1,0:T(8,128)} fusion(f32[128,128]{1,0:T(8,128)S(1)} %get-tuple-element.57, f32[128,128]{1,0:T(8,128)S(1)} %get-tuple-element.56, f32[128,128]{1,0:T(8,128)S(1)} %get-tuple-element.55, f32[128,128]{1,0:T(8,128)S(1)} %get-tuple-element.54), kind=kLoop, calls=%fused_computation.56 | loop fusion | flops 262144 | bytes 524288 | tf_op jit(solution)/shard_map/mul | solution.py:453
  (32 shorter events, 0.7 us)
Async XLA Ops:
  0.6 1.0 %copy-start = (bf16[1,256,8,128]{3,2,1,0:T(8,128)(2,1)S(1)}, bf16[1,256,8,128]{3,2,1,0:T(8,128)(2,1)}, u32[]{:S(2)}) copy-start(bf16[1,256,8,128]{3,2,1,0:T(8,128)(2,1)} %param.9) | copy-start | bytes 1572868
  3.6 33.1 %copy-start.3 = (bf16[3,3,128]{2,1,0:T(4,128)(2,1)S(1)}, bf16[3,3,128]{2,1,0:T(4,128)(2,1)}, u32[]{:S(2)}) copy-start(bf16[3,3,128]{2,1,0:T(4,128)(2,1)} %param.15) | copy-start | bytes 6916
  9.0 1.0 %copy-start.1 = (bf16[1,1024,128]{2,1,0:T(8,128)(2,1)S(1)}, bf16[1,1024,128]{2,1,0:T(8,128)(2,1)}, u32[]{:S(2)}) copy-start(bf16[1,1024,128]{2,1,0:T(8,128)(2,1)} %param.17) | copy-start | bytes 786436
  40.1 1.5 %copy-start.2 = (bf16[1024,512]{1,0:T(8,128)(2,1)S(1)}, bf16[1024,512]{1,0:T(8,128)(2,1)}, u32[]{:S(2)}) copy-start(bf16[1024,512]{1,0:T(8,128)(2,1)} %get-tuple-element.11) | copy-start | bytes 3145732

commit v5 on v4

--- a/solution.py
+++ b/solution.py
@@ -163,7 +163,6 @@
     own_ref,
     source_ref,
     weights_ref,
-    column_ref,
     in_ref,
     full_ref,
     mapped_ref,
@@ -186,15 +185,18 @@
 
     def remap():
         shape = (terms, terms)
-        source = column_ref[...]
-        earlier = lax.broadcasted_iota(jnp.int32, shape, 1) <= lax.broadcasted_iota(
-            jnp.int32, shape, 0
-        )
-        same = (source == source_ref[...]) & earlier
+        here = lax.axis_index("tile")
+        tiles = lax.broadcasted_iota(jnp.int32, source_ref.shape, 0)
+        named = jnp.where(tiles == here, source_ref[...].astype(jnp.float32), 0.0)
+        row = jnp.sum(named, axis=0, keepdims=True)
+        across = lax.broadcasted_iota(jnp.int32, shape, 1)
+        down = lax.broadcasted_iota(jnp.int32, shape, 0)
+        source = jnp.sum(jnp.where(across == down, row, 0.0), axis=1, keepdims=True)
+        same = (source == row) & (across <= down)
         rank = jnp.sum(jnp.where(same, 1.0, 0.0), axis=1, keepdims=True) - 1.0
         capacity = filled // lax.axis_size("tile")
-        slot = source.astype(jnp.float32) * capacity + rank
-        slot = jnp.where(source >= 0, slot, -1.0)
+        slot = source * capacity + rank
+        slot = jnp.where(source >= 0.0, slot, -1.0)
         ids = lax.broadcasted_iota(jnp.int32, (terms, filled), 1).astype(jnp.float32)
         pick_ref[...] = jnp.where(slot == ids, 1.0, 0.0).astype(jnp.bfloat16)
         wait_all(copies)
@@ -314,7 +316,7 @@
         compiler_params=pltpu.CompilerParams(
             collective_id=collective_id,
             has_side_effects=True,
-            vmem_limit_bytes=52 * 2**20,
+            vmem_limit_bytes=49 * 2**20,
         ),
     )(*operands)
 
@@ -352,11 +354,7 @@
     send_pick = (slot_block[:, None] == blocks[None, :]).astype(jnp.bfloat16)
     outgoing = jnp.einsum("nb,abkc->ankc", send_pick, latlon, preferred_element_type=jnp.float32)
     outgoing = outgoing.astype(jnp.bfloat16)
-    tile_mask = (jnp.arange(tile_total) == tile_now)[:, None]
-    own_source = jnp.sum(jnp.where(tile_mask, term_source, 0), axis=0)
-    own_count = jnp.sum(jnp.where(tile_mask[:, 0], term_count, 0))
-    own_use = positions < own_count
-    named = jnp.where(own_use, own_source, -1)
+    named = jnp.where(in_use, term_source, -1)
     weights = remap_weights[0]
     ext_cells = weights.shape[0]
     term_pts = weights.shape[1]
@@ -383,9 +381,8 @@
         0,
         outgoing,
         upstream,
-        named[None, :],
+        named,
         weights,
-        named[:, None],
     )
     field = remapped.reshape(batch_rows, ext_edge, ext_edge, chan_local)
     turn = rotation[0]

time: 70.6 us -> 61.9 us (0.88)
  other arithmetic: 8.21 us -> 5.6 us
  Pallas kernels: 49.3 us -> 46.8 us
  matrix products: 5.5 us -> 3.04 us
  local copies, waits for them, and re-layouts: 5.67 us -> 4.62 us
    pallas_call x2, Pallas kernels: 49.3 us -> 46.8 us  [call(): pl.pallas_call(kernel, out_shape=[jax.ShapeDtypeStruct(*one) for one in s...]
    reduce_sum x2 -> x0, other arithmetic: 2.07 us -> none  [the longest x1 1.29 us: body(): own_count = jnp.sum(jnp.where(tile_mask[:, 0], term_count, 0))]
    dot_general x1, matrix products: 2.37 us -> 1.15 us  [body(): mixed = jnp.dot(active_all, own_cols, preferred_element_type=jnp.float32)]
    dot_general x1, matrix products: 1.66 us -> 0.44 us  [body(): lax.dot_general(piece, own_rows, (((1,), (1,)), ((), ())), preferred_elem...]
    convert_element_type x1, local copies, waits for them, and re-layouts: 1.44 us -> 0.51 us  [body(): outgoing = outgoing.astype(jnp.bfloat16)]
where the time goes in v5:
time: 61.9 us; the launch traced here: 61.5 us
  Pallas kernels  46.8 us (76%)
  other arithmetic  5.6 us (9%)
  local copies, waits for them, and re-layouts  4.62 us (7%)
  matrix products  3.04 us (5%)
  between operations  1.5 us (2%)
    pallas_call x2, Pallas kernels, call(): pl.pallas_call(kernel, out_shape=[jax.ShapeDtypeStruct(*one) for one in s...  46.8 us
    unnamed x9, local copies, waits for them, and re-layouts  3.07 us

profile of v5, /device:TPU:0, one launch (start us, length us, event | category | flops | bytes accessed | tf_op | source)
XLA Modules:
  0.0 61.5 jit_solution(8027453278279788769)
XLA Ops:
  0.6 1.0 %copy-done = bf16[1,256,8,128]{3,2,1,0:T(8,128)(2,1)S(1)} copy-done((bf16[1,256,8,128]{3,2,1,0:T(8,128)(2,1)S(1)}, bf16[1,256,8,128]{3,2,1,0:T(8,128)(2,1)}, u32[]{:S(2)}) %copy-start) | copy-done | bytes 524312
  1.7 0.7 %broadcast_add_fusion = s32[8,256]{1,0:T(8,128)S(1)} fusion(s32[8,256]{1,0:T(8,128)} %param.12), kind=kLoop, calls=%fused_computation.82 | loop fusion | flops 2048 | bytes 16384 | tf_op jit(solution)/shard_map/add | solution.py:352
  2.4 0.8 %fusion.33 = pred[8,256]{1,0:T(8,128)(4,1)S(1)} fusion(s32[8,256]{1,0:T(8,128)} %param.11, s32[]{:T(128)S(6)} %axis_index.23, s32[8]{0:T(128)} %param.13), kind=kLoop, calls=%fused_computation.75 | loop fusion | flops 6144 | bytes 10276 | tf_op jit(solution)/shard_map/and | solution.py:346
  3.2 0.1 fusion.3
  3.3 0.2 select_reduce_fusion
  3.6 0.1 sub.15
  3.6 0.4 fusion
  4.1 0.5 copy.72
  4.6 0.8 %fusion.32.source_ref = s32[8,256]{1,0:T(8,128)S(1)} fusion(s32[8,256]{1,0:T(8,128)} %param.11, s32[8]{0:T(128)} %param.13), kind=kLoop, calls=%fused_computation.74 | loop fusion | flops 4096 | bytes 16416 | tf_op jit(solution)/shard_map/jit(_where)/select_n | solution.py:357
  5.4 0.9 %copy-done.1 = bf16[1,1024,128]{2,1,0:T(8,128)(2,1)S(1)} copy-done((bf16[1,1024,128]{2,1,0:T(8,128)(2,1)S(1)}, bf16[1,1024,128]{2,1,0:T(8,128)(2,1)}, u32[]{:S(2)}) %copy-start.1) | copy-done | bytes 262168
  6.3 25.1 %shard_map.120 = (bf16[3072,128]{1,0:T(8,128)(2,1)}, bf16[1024,512]{1,0:T(8,128)(2,1)S(1)}, bf16[1156,128]{1,0:T(8,128)(2,1)S(1)}, bf16[256,384]{1,0:T(8,128)(2,1)S(1)}) custom-call(bf16[3072,128]{1,0:T(8,128)(2,1)S(1)} %bitcast.81, bf16[1024,128]{1,0:T(8,128)(2,1)S(1)} %bitcast.85, s32[8,256]{1,0:T(8,128)S(1)} %fusion.32.source_ref, bf16[1156,2048]{1,0:T(8,128)(2,1)} %bitcast.86), custom_call_target="tpu_custom_call" | custom-call | tf_op jit(solution)/shard_map/pallas_call | solution.py:300
  31.5 0.1 reshape.98
  32.4 0.4 fusion.30
  32.8 0.9 %fusion.13 = (f32[128]{0:T(128)S(1)}, f32[128]{0:T(128)S(1)}, f32[128]{0:T(128)S(1)}, f32[128]{0:T(128)S(1)}, f32[128]{0:T(128)S(1)}, /*index=5*/f32[128]{0:T(12...) fusion(bf16[1,34,34,128]{3,2,1,0:T(8,128)(2,1)S(1)} %reshape.98, ...), kind=kLoop, calls=%fused_computation.37 | loop fusion | flops 6814592 | bytes 3941376 | tf_op jit(solution)/shard_map/reduce_sum | solution.py:43
  33.7 0.7 %broadcast_multiply_fusion.8 = (f32[1,32,32,128]{3,2,1,0:T(8,128)S(1)}, f32[1,32,32,128]{3,2,1,0:T(8,128)S(1)}, f32[1,32,32,128]{3,2,1,0:T(8,128)S(1)}, f32[1,32...) fusion(f32[1,32,32,128]{3,2,1,0:T(8,128)S(1)} %get-tuple-elemen, ...), kind=kLoop, calls=%fused_computation.66 | loop fusion | flops 1835008 | bytes 6033920 | tf_op jit(solution)/shard_map/mul | solution.py:44
  34.4 0.7 %add_convert_fusion = bf16[1,34,34,128]{3,2,1,0:T(8,128)(2,1)S(1)} fusion(f32[1,32,32,128]{3,2,1,0:T(8,128)S(1)} %get-tuple-element.38, f32[1,32,32,128]{3,2,1,0:T(8,128)S(1)} %get-tuple-element.39, f32[1,32,32,128]{3,2,1,0:T(8,128)S(1)} %get-tuple-element.40, f32[1,32,32,128]{3,2,1,0:T(8,128)S(1)} %get-tuple-element.41, ...), kind=kLoop, calls=%fused_computation.10 | loop fusion | flops 1331712 | bytes 5014528 | tf_op jit(solution)/shard_map/convert_element_type | solution.py:405
  35.1 0.1 reshape.99.grad_ref
  35.2 0.3 fusion.42
  35.8 21.6 %shard_map.121 = (bf16[3072,128]{1,0:T(8,128)(2,1)S(1)}, bf16[1024,512]{1,0:T(8,128)(2,1)S(1)}, bf16[512,128]{1,0:T(8,128)(2,1)S(1)}, f32[16,128]{1,0:T(8,128)S(1)}) custom-call(bf16[1156,128]{1,0:T(8,128)(2,1)S(1)} %reshape.99.grad_ref, bf16[1024,128]{1,0:T(8,128)(2,1)S(1)} %bitcast.83, bf16[256,384]{1,0:T(8,128)(2,1)S(1)} %get-tuple-element.13.pick_ref, ...), custom_call_target="tpu_custom_call" | custom-call | tf_op jit(solution)/shard_map/pallas_call | solution.py:300
  57.4 1.2 %fusion.2 = bf16[1,1024,128]{2,1,0:T(8,128)(2,1)} fusion(bf16[1024,512]{1,0:T(8,128)(2,1)S(1)} %get-tuple-element.14, bf16[512,512]{1,0:T(8,128)(2,1)S(1)} %copy-done.2, s32[]{:T(128)S(6)} %select_n.71), kind=kOutput, calls=%fused_computation.5 | convolution fusion | flops 134348800 | bytes 1441796 | tf_op jit(solution)/shard_map/dot_general | solution.py:439
  58.5 0.6 fusion.1
  59.1 1.1 %copy.42 = bf16[1,256,8,128]{3,2,1,0:T(8,128)(2,1)} copy(bf16[1,256,8,128]{1,3,2,0:T(8,128)(2,1)S(1)} %fusion.1) | data formatting | bytes 1048576
  60.2 0.6 mul.255
  60.8 0.7 %maximum_multiply_fusion = f32[128,512]{1,0:T(8,128)} fusion(f32[128,128]{1,0:T(8,128)S(1)} %get-tuple-element.53, f32[128,128]{1,0:T(8,128)S(1)} %get-tuple-element.52, f32[128,128]{1,0:T(8,128)S(1)} %get-tuple-element.51, f32[128,128]{1,0:T(8,128)S(1)} %get-tuple-element.50), kind=kLoop, calls=%fused_computation.56 | loop fusion | flops 262144 | bytes 524288 | tf_op jit(solution)/shard_map/mul | solution.py:450
  (27 shorter events, 0.3 us)
Async XLA Ops:
  0.6 1.0 %copy-start = (bf16[1,256,8,128]{3,2,1,0:T(8,128)(2,1)S(1)}, bf16[1,256,8,128]{3,2,1,0:T(8,128)(2,1)}, u32[]{:S(2)}) copy-start(bf16[1,256,8,128]{3,2,1,0:T(8,128)(2,1)} %param.9) | copy-start | bytes 1572868
  1.7 29.9 %copy-start.3 = (bf16[3,3,128]{2,1,0:T(4,128)(2,1)S(1)}, bf16[3,3,128]{2,1,0:T(4,128)(2,1)}, u32[]{:S(2)}) copy-start(bf16[3,3,128]{2,1,0:T(4,128)(2,1)} %param.15) | copy-start | bytes 6916
  3.6 28.7 %copy-start.2 = (bf16[512,512]{1,0:T(8,128)(2,1)S(1)}, bf16[512,512]{1,0:T(8,128)(2,1)}, u32[]{:S(2)}) copy-start(bf16[512,512]{1,0:T(8,128)(2,1)} %param.16) | copy-start | bytes 1572868
  5.4 1.0 %copy-start.1 = (bf16[1,1024,128]{2,1,0:T(8,128)(2,1)S(1)}, bf16[1,1024,128]{2,1,0:T(8,128)(2,1)}, u32[]{:S(2)}) copy-start(bf16[1,1024,128]{2,1,0:T(8,128)(2,1)} %param.17) | copy-start | bytes 786436
